TPU v7x, 256 devices: a whole 4x4x8 slice. The times are simulated.
256 devices in a mesh: bulk: 16 (over z_hi, y, core), tensor: 16 (over z_lo, x).
Axes of the slice: x: 4, y: 4, z: 8 (z_hi: 2, z_lo: 4; z = z_hi * 4 + z_lo), core: 2. Of those that a mesh axis runs over, the one named last changes fastest.
Arguments:
- spectrum: bfloat16 [256, 2, 163840], P('tensor', None, 'bulk'), may hold values from -6 to 6
- out_grad: bfloat16 [256, 2, 163840], P('tensor', None, 'bulk'), may hold values from -6 to 6
- in_factor: bfloat16 [256, 1024], P(None, 'tensor'), may hold values from -0.375 to 0.375
- out_factor: bfloat16 [256, 1024], P(None, 'tensor'), may hold values from -0.375 to 0.375
- mode_factor: bfloat16 [1024, 2, 163840], P('tensor', None, 'bulk'), may hold values from -6 to 6
Outputs:
- grad_spectrum: bfloat16 [256, 2, 163840], P('tensor', None, 'bulk')
- grad_modes: bfloat16 [1024, 2, 163840], P('tensor', None, 'bulk')
- grad_in_factor: float32 [256, 1024], P(None, 'tensor')
- grad_out_factor: float32 [256, 1024], P(None, 'tensor')
All inputs are finite; a program needn't handle non-finite values.
Results may differ from a plain program's by a relative error of at most 0.023.
Values may be sent and summed in bfloat16 or wider, within the bound.
No kernel may reach another device: no remote copies, remote signals or barrier semaphores. Data moves between devices by JAX's collectives and lax.ppermute only.
A program may use at most 128 MiB of HBM per device.

v0:
```python
import jax
import jax.numpy as jnp
from jax import lax
from jax.sharding import PartitionSpec as P


def pointwise(mode_part, u, v):
    mode_f = mode_part.astype(jnp.float32)
    m0, m1 = (mode_f[:, 0], mode_f[:, 1])
    u0, u1 = (u[:, 0], u[:, 1])
    v0, v1 = (v[:, 0], v[:, 1])
    pulled = jnp.stack([v0 * m0 + v1 * m1, v1 * m0 - v0 * m1], axis=1).astype(jnp.bfloat16)
    mode_grad = jnp.stack([v0 * u0 + v1 * u1, v1 * u0 - v0 * u1], axis=1).astype(jnp.bfloat16)
    return (pulled, mode_grad)


def weigh(mode_part, u):
    mode_f = mode_part.astype(jnp.float32)
    m0, m1 = (mode_f[:, 0], mode_f[:, 1])
    u0, u1 = (u[:, 0], u[:, 1])
    return jnp.stack([m0 * u0 - m1 * u1, m0 * u1 + m1 * u0], axis=1).astype(jnp.bfloat16)


def on_device(spectrum, out_grad, in_factor, out_factor, mode_factor):
    scale = float(mode_factor.shape[2] * lax.axis_size("bulk")) ** (-0.5)
    whole = lax.all_gather(spectrum, "tensor", axis=0, tiled=True)
    u = jnp.einsum("cr,ctk->rtk", in_factor, whole, preferred_element_type=jnp.float32)
    weighted = weigh(mode_factor, u)
    piece = lax.all_gather(out_grad, "tensor", axis=0, tiled=True)
    rows = out_factor
    total = jnp.einsum("or,otk->rtk", rows, piece, preferred_element_type=jnp.float32)
    block = scale * jnp.einsum("otk,rtk->or", piece, weighted, preferred_element_type=jnp.float32)
    pulled, grad_modes = pointwise(mode_factor, u, total)
    rows = in_factor
    grad_spectrum = lax.psum_scatter(
        jnp.einsum("cr,rtk->ctk", rows, pulled, preferred_element_type=jnp.float32).astype(
            jnp.bfloat16
        ),
        "tensor",
        scatter_dimension=0,
        tiled=True,
    )
    in_part = scale * jnp.einsum("ctk,rtk->cr", whole, pulled, preferred_element_type=jnp.float32)
    grad_in_factor, grad_out_factor = (
        lax.psum(in_part.astype(jnp.bfloat16), "bulk").astype(jnp.float32),
        lax.psum(block.astype(jnp.bfloat16), "bulk").astype(jnp.float32),
    )
    return (grad_spectrum, grad_modes, grad_in_factor, grad_out_factor)


def solution(mesh):
    return jax.shard_map(
        on_device,
        mesh=mesh,
        in_specs=(
            P("tensor", None, "bulk"),
            P("tensor", None, "bulk"),
            P(None, "tensor"),
            P(None, "tensor"),
            P("tensor", None, "bulk"),
        ),
        out_specs=(
            P("tensor", None, "bulk"),
            P("tensor", None, "bulk"),
            P(None, "tensor"),
            P(None, "tensor"),
        ),
        check_vma=False,
    )
```

profile of v0, /device:TPU:1, one launch (start us, length us, event | category | flops | bytes accessed | tf_op | source)
XLA Modules:
  0.0 703.6 jit_solution(7889313247921128201)
XLA Ops:
  7.2 2.3 copy.17
  9.6 2.1 copy.14
  11.8 3.2 copy_convert_fusion
  15.0 122.7 %all-gather.5.cloned.1.call-done = bf16[256,2,10240]{2,0,1:T(8,128)(2,1)} async-done(((bf16[16,2,10240]{2,0,1:T(8,128)(2,1)}), bf16[256,2,10240]{2,0,1:T(8,128)(2,1)}) %all-gather.5.cloned.1.call-update) | async-done | bytes 10485776 | tf_op jit(solution)/shard_map/all_gather | solution.py:26
  137.7 8.3 %fusion.22 = f32[64,2,10240]{2,0,1:T(8,128)} fusion(bf16[256,2,10240]{2,0,1:T(8,128)(2,1)} %all-gather.5.cloned.1.call-done, bf16[256,64]{0,1:T(8,128)(2,1)S(1)} %copy-done), kind=kOutput, calls=%fused_computation.24 | convolution fusion | flops 671088640 | bytes 15761408 | tf_op jit(solution)/shard_map/cr,ctk->rtk/dot_general | solution.py:27
  146.0 114.4 %all-gather.3.cloned.1.call-done = bf16[256,2,10240]{2,0,1:T(8,128)(2,1)} async-done(((bf16[16,2,10240]{2,0,1:T(8,128)(2,1)}), bf16[256,2,10240]{2,0,1:T(8,128)(2,1)}) %all-gather.3.cloned.1.call-update) | async-done | bytes 10485776 | tf_op jit(solution)/shard_map/all_gather | solution.py:29
  260.4 6.1 fusion.25
  266.5 0.9 copy-done.3
  267.5 2.4 subtract_convert_fusion
  269.9 1.5 copy-done.2
  271.4 1.2 slice-done.1
  272.6 0.7 slice-done.2
  273.3 3.9 fusion.21
  277.3 7.9 %fusion.18 = bf16[256,64]{0,1:T(8,128)(2,1)} fusion(bf16[256,2,10240]{2,0,1:T(8,128)(2,1)} %all-gather.3.cloned.1.call-done, bf16[64,1,10240]{2,0,1:T(8,128)(2,1)S(1)} %copy-done.5, bf16[64,1,10240]{2,0,1:T(8,128)(2,1)S(1)} %copy-done.4), kind=kOutput, calls=%fused_computation.22 | convolution fusion | flops 672432128 | bytes 13139968 | tf_op jit(solution)/shard_map/otk,rtk->or/dot_general | solution.py:32
  285.4 5.4 fusion
  290.8 26.6 %copy.16 = bf16[256,2,10240]{2,1,0:T(2,128)(2,1)} copy(bf16[256,2,10240]{0,2,1:T(8,128)(2,1)} %fusion) | data formatting | bytes 20971520 | tf_op jit(solution)/shard_map/convert_element_type | solution.py:36
  317.4 0.6 copy-done.8
  319.3 4.8 add_convert_fusion.1
  324.4 4.2 copy.18
  328.6 118.1 %all-reduce.7.cloned.1.call-done = (bf16[256,64]{0,1:T(8,128)(2,1)}, bf16[256,64]{0,1:T(8,128)(2,1)}) async-done(((bf16[256,64]{0,1:T(8,128)(2,1)}, bf16[256,64]{0,1:T(8,128)(2,1)}), (bf16[256,64]{0,1:T(8,128)(2,1)}, bf16[256,64]{0,1:T(8,128)(2,1)})) %all-reduce.7.cloned.1.call-update) | async-done | bytes 65552 | tf_op jit(solution)/shard_map/psum | solution.py:45
  446.7 1.4 convert_element_type.36
  448.1 1.4 convert_element_type.39
  449.5 245.2 %all-reduce.5.cloned.1.call-done = bf16[256,2,10240]{2,1,0:T(2,128)(2,1)} async-done(((bf16[256,2,10240]{2,1,0:T(2,128)(2,1)}), bf16[256,2,10240]{2,1,0:T(2,128)(2,1)}) %all-reduce.5.cloned.1.call-update) | async-done | bytes 10485776
  694.7 2.4 constant_dynamic-slice_fusion
  (30 shorter events, 1.3 us)
Async XLA Ops:
  7.2 130.6 %copy-start = (bf16[256,64]{0,1:T(8,128)(2,1)S(1)}, bf16[256,64]{0,1:T(8,128)(2,1)}, u32[]{:S(2)}) copy-start(bf16[256,64]{0,1:T(8,128)(2,1)} %param.7) | copy-start | bytes 98308
  7.2 4.6 copy-start.6
  7.2 130.5 %all-gather.5.cloned.1.call-start = ((), (), s32[]{:S(2)}) async-start(), calls=%async_computation.1 | async-start | bytes 11141120 | tf_op jit(solution)/shard_map/all_gather | solution.py:26
  9.5 250.9 %all-gather.3.cloned.1.call-start = ((), (), s32[]{:S(2)}) async-start(), calls=%async_computation | async-start | bytes 11141120 | tf_op jit(solution)/shard_map/all_gather | solution.py:29
  11.7 435.0 %all-reduce.7.cloned.1.call-start = ((), (), s32[]{:S(2)}) async-start(), calls=%async_computation.3 | async-start | bytes 131072 | tf_op jit(solution)/shard_map/psum | solution.py:45
  15.0 245.4 %copy-start.7 = (bf16[256,64]{0,1:T(8,128)(2,1)S(1)}, bf16[256,64]{0,1:T(8,128)(2,1)}, u32[]{:S(2)}) copy-start(bf16[256,64]{0,1:T(8,128)(2,1)} %param.8) | copy-start | bytes 98308
  260.4 6.1 copy-start.1
  260.4 7.0 %copy-start.3 = (f32[64,2,10240]{2,0,1:T(8,128)S(1)}, f32[64,2,10240]{2,0,1:T(8,128)}, u32[]{:S(2)}) copy-start(f32[64,2,10240]{2,0,1:T(8,128)} %copy_convert_fusion) | copy-start | bytes 15728644
  260.4 11.0 %slice-start = ((s8[10485760]{0:T(1024)(128)(4,1)}), s8[4194304]{0:T(1024)(128)(4,1)S(1)}, s32[]{:S(2)}) async-start(s8[10485760]{0:T(1024)(128)(4,1)} %bitcast.35), calls=%async_computation.4 | async-start | bytes 8388608
  260.4 12.2 %slice-start.1 = ((s8[10485760]{0:T(1024)(128)(4,1)}), s8[4194304]{0:T(1024)(128)(4,1)S(1)}, s32[]{:S(2)}) async-start(s8[10485760]{0:T(1024)(128)(4,1)} %bitcast.35), calls=%async_computation.5 | async-start | bytes 8388608
  267.5 3.9 copy-start.2
  267.5 5.9 slice-start.2
  273.3 3.9 copy-start.4
  273.3 3.9 copy-start.5
  285.2 409.5 %all-reduce.5.cloned.1.call-start = ((), (), s32[]{:S(2)}) async-start(), calls=%async_computation.2 | async-start | bytes 20971520
  317.4 0.7 copy-start.8
Sparse Core Ops, SparseCore 0:
  10.4 127.2 all-gather.4
  140.1 120.2 all-gather.2
  285.3 161.3 all-reduce.6
  449.4 245.2 all-reduce.4
where the time goes:
time: 705 us; the launch traced here: 704 us
  waiting for transfers between devices  600 us (85%)
  local copies, waits for them, and re-layouts  43.2 us (6%)
  matrix products  31.6 us (4%)
  between operations  14.5 us (2%)
  other arithmetic  13.5 us (2%)
    unnamed x5, waiting for transfers between devices  245 us
    all_gather x1, waiting for transfers between devices, on_device(): whole = lax.all_gather(spectrum, 'tensor', axis=0, tiled=True)  123 us
    psum x1, waiting for transfers between devices, on_device(): lax.psum(in_part.astype(jnp.bfloat16), 'bulk').astype(jnp.float32)  118 us
    all_gather x1, waiting for transfers between devices, on_device(): piece = lax.all_gather(out_grad, 'tensor', axis=0, tiled=True)  114 us
    convert_element_type x1, local copies, waits for them, and re-layouts, on_device(): jnp.einsum('cr,rtk->ctk', rows, pulled, preferred_element_type=jnp.float32)  26.6 us
    unnamed x29, local copies, waits for them, and re-layouts  16.6 us
  transfers between devices with their start and end apart: 4, of which 4 were waited for; matrix products, arithmetic and copies ran while one was open for 8% of the time, Pallas kernels for 0%

commit v1 on v0

v1 whole, which is shorter than its diff:
```python
import functools

import jax
import jax.numpy as jnp
from jax import lax
from jax.experimental import pallas as pl
from jax.experimental.pallas import tpu as pltpu
from jax.sharding import PartitionSpec as P

BF = jnp.bfloat16
F32 = jnp.float32
NX = 4
NZ = 4
ORDER = ((0, 1, 2, 3), (1, 0, 2, 3), (2, 3, 1, 0), (3, 2, 1, 0))


def x_shift(step):
    return [(z * NX + x, z * NX + (x + step) % NX) for z in range(NZ) for x in range(NX)]


def z_moves(pairs):
    return [(a * NX + x, b * NX + x) for a, b in pairs for x in range(NX)]


SWAP = z_moves([(0, 1), (1, 0), (2, 3), (3, 2)])
MIDDLE = z_moves([(1, 2), (2, 1)])
OUTWARD = z_moves([(1, 0), (2, 3)])
INWARD = z_moves([(0, 1), (3, 2)])


def send(a, moves):
    return lax.ppermute(a, "tensor", moves)


def send_bulk(a, move):
    return lax.ppermute(a, "bulk", [(i, move(i)) for i in range(16)])


def y_shift(step):
    return lambda i: (i // 8) * 8 + ((i // 2 % 4 + step) % 4) * 2 + i % 2


def nt_dot(a, b):
    return lax.dot_general(a, b, (((1,), (1,)), ((), ())), preferred_element_type=F32)


def nn_dot(a, b):
    return jnp.dot(a, b, preferred_element_type=F32)


def body(steps, info, *refs):
    spec, grad, mode, fac = refs[0:6], refs[6:12], refs[12:16], refs[16:20]
    gm, gs, d_in, d_out = refs[20:24], refs[24:28], refs[28], refs[29]
    f_in, ft_in, ft_out, tmp, acc_in, acc_out = refs[30:]
    k = pl.program_id(0)
    middle = info[16] == 1

    @pl.when(k == 0)
    def _():
        for which, rows, cols in ((0, f_in, ft_in), (1, None, ft_out)):
            whole = jnp.concatenate([f[which] for f in fac], axis=0).astype(F32)
            tmp[...] = whole.T
            for i in range(16):
                src = pl.ds(pl.multiple_of(info[i] * 16, 16), 16)
                acc_in[16 * i : 16 * i + 16, :] = tmp[src, :]
            if rows is not None:
                rows[...] = acc_in[...].astype(BF)
            cols[...] = acc_in[...].T.astype(BF)
        acc_in[...] = jnp.zeros_like(acc_in)
        acc_out[...] = jnp.zeros_like(acc_out)

    def gathered(parts, t):
        own, near, c_mid, c_end, d_mid, d_end = (p[t] for p in parts)
        return jnp.concatenate(
            [own, near, jnp.where(middle, c_mid, c_end), jnp.where(middle, d_mid, d_end)], axis=0
        )

    s = [gathered(spec, t) for t in range(2)]
    g = [gathered(grad, t) for t in range(2)]
    m0, m1 = [jnp.concatenate([m[t] for m in mode], axis=0).astype(F32) for t in range(2)]
    u0, u1 = [nn_dot(ft_in[...], a) for a in s]
    v0, v1 = [nn_dot(ft_out[...], a) for a in g]
    w = [(m0 * u0 - m1 * u1).astype(BF), (m0 * u1 + m1 * u0).astype(BF)]
    p = [(v0 * m0 + v1 * m1).astype(BF), (v1 * m0 - v0 * m1).astype(BF)]
    q = [(v0 * u0 + v1 * u1).astype(BF), (v1 * u0 - v0 * u1).astype(BF)]
    for t in range(2):
        part = nn_dot(f_in[...], p[t]).astype(BF)
        for i in range(4):
            gm[i][t] = q[t][64 * i : 64 * i + 64, :]
            gs[i][t] = part[64 * i : 64 * i + 64, :]
    acc_in[...] += nt_dot(s[0], p[0]) + nt_dot(s[1], p[1])
    acc_out[...] += nt_dot(g[0], w[0]) + nt_dot(g[1], w[1])

    @pl.when(k == steps - 1)
    def _():
        for acc, out in ((acc_in, d_in), (acc_out, d_out)):
            for i in range(16):
                dst = pl.ds(pl.multiple_of(info[i] * 16, 16), 16)
                tmp[dst, :] = acc[16 * i : 16 * i + 16, :]
            out[...] = tmp[...].T


def compute(info, spec, grad, mode, fac, tile=512):
    modes = mode[0].shape[2]
    steps = modes // tile
    block = (2, 64, tile)
    here = pl.BlockSpec(block, lambda k, n: (0, 0, k))
    mid = pl.BlockSpec(block, lambda k, n: (0, 0, k * n[16]))
    end = pl.BlockSpec(block, lambda k, n: (0, 0, k * (1 - n[16])))
    gathered = [here, here, mid, end, mid, end]
    whole = pl.BlockSpec((2, 64, 256), lambda k, n: (0, 0, 0))
    square = pl.BlockSpec((256, 256), lambda k, n: (0, 0))
    piece = jax.ShapeDtypeStruct((2, 64, modes), BF)
    factor = jax.ShapeDtypeStruct((256, 256), F32)
    outs = pl.pallas_call(
        functools.partial(body, steps),
        grid_spec=pltpu.PrefetchScalarGridSpec(
            num_scalar_prefetch=1,
            grid=(steps,),
            in_specs=gathered * 2 + [here] * 4 + [whole] * 4,
            out_specs=[here] * 8 + [square] * 2,
            scratch_shapes=[pltpu.VMEM((256, 256), BF)] * 3 + [pltpu.VMEM((256, 256), F32)] * 3,
        ),
        out_shape=[piece] * 8 + [factor] * 2,
        compiler_params=pltpu.CompilerParams(vmem_limit_bytes=40 * 1024 * 1024),
        cost_estimate=pl.CostEstimate(
            flops=20 * 256 * 256 * modes, bytes_accessed=10 * 256 * 2 * modes * 2, transcendentals=0
        ),
    )(info, *spec, *grad, *mode, *fac)
    return outs[0:4], outs[4:8], outs[8], outs[9]


def cut(a, x, d, size):
    start = ((x + d) % NX) * size
    return lax.dynamic_slice_in_dim(a, start, size, axis=2)


def scatter_x(a, x):
    size = a.shape[2] // NX
    parts = [cut(a, x, d, size) for d in range(NX)]
    return [parts[0]] + [send(parts[d], x_shift(d)) for d in range(1, NX)]


def collect_x(parts, x):
    size = parts[0].shape[2]
    parts = [parts[0]] + [send(parts[d], x_shift(-d)) for d in range(1, NX)]
    out = jnp.zeros(parts[0].shape[:2] + (size * NX,), BF)
    for d in range(NX):
        out = lax.dynamic_update_slice_in_dim(out, parts[d], ((x + d) % NX) * size, axis=2)
    return out


def gather_z(own):
    near = send(own, SWAP)
    c_mid = send(own, MIDDLE)
    d_mid = send(near, MIDDLE)
    c_end = send(c_mid, OUTWARD)
    d_end = send(d_mid, OUTWARD)
    return [own, near, c_mid, c_end, d_mid, d_end]


def add(a, b):
    return (a.astype(F32) + b.astype(F32)).astype(BF)


def scatter_z(own, near, c, d):
    d = add(d, send(d, INWARD))
    c = add(c, send(c, INWARD))
    near = add(near, send(d, MIDDLE))
    from_c = send(c, MIDDLE)
    from_near = send(near, SWAP)
    return (own.astype(F32) + from_c.astype(F32) + from_near.astype(F32)).astype(BF)


def on_device(spectrum, out_grad, in_factor, out_factor, mode_factor):
    scale = float(mode_factor.shape[2] * lax.axis_size("bulk")) ** (-0.5)
    place = lax.axis_index("tensor")
    x, z = place % NX, place // NX
    order = jnp.asarray(ORDER, jnp.int32)[z]
    blocks = order[:, None] * NX + (x - jnp.arange(NX, dtype=jnp.int32)[None, :]) % NX
    middle = ((z == 1) | (z == 2)).astype(jnp.int32)
    info = jnp.concatenate([blocks.reshape(16), middle[None]])

    turn = lambda a: jnp.transpose(a, (1, 0, 2))
    own_s = jnp.concatenate(scatter_x(turn(spectrum), x), axis=1)
    own_g = jnp.concatenate(scatter_x(turn(out_grad), x), axis=1)
    factors = jnp.stack([in_factor.T, out_factor.T])
    fac = [factors] + [send(factors, x_shift(d)) for d in range(1, NX)]
    spec = gather_z(own_s)
    grad = gather_z(own_g)
    mode_factor, _ = lax.optimization_barrier((mode_factor, own_g))
    mode = scatter_x(turn(mode_factor), x)

    gm, gs, d_in, d_out = compute(info, spec, grad, mode, fac)

    grad_spectrum = scatter_z(*gs)
    grad_modes = turn(collect_x(gm, x))
    grad_spectrum = collect_x([grad_spectrum[:, 16 * d : 16 * d + 16] for d in range(NX)], x)

    both = jnp.stack([d_in, d_out]).reshape(2, NX, 64, 256)
    total = both[:, 0]
    for d in range(1, NX):
        total = total + send(both[:, d], x_shift(-d))
    total = total + send_bulk(total, lambda i: i ^ 1)
    total = (total + send_bulk(total, y_shift(2))) + (
        send_bulk(total, y_shift(1)) + send_bulk(total, y_shift(3))
    )
    total = scale * (total + send_bulk(total, lambda i: i ^ 8))
    return (turn(grad_spectrum), grad_modes, total[0].T, total[1].T)


def solution(mesh):
    return jax.shard_map(
        on_device,
        mesh=mesh,
        in_specs=(
            P("tensor", None, "bulk"),
            P("tensor", None, "bulk"),
            P(None, "tensor"),
            P(None, "tensor"),
            P("tensor", None, "bulk"),
        ),
        out_specs=(
            P("tensor", None, "bulk"),
            P("tensor", None, "bulk"),
            P(None, "tensor"),
            P(None, "tensor"),
        ),
        check_vma=False,
    )
```

time: 705 us -> 232 us (0.33)
  waiting for transfers between devices: 600 us -> 120 us
  starting transfers between devices: 0.34 us -> 83.1 us
  local copies, waits for them, and re-layouts: 43.2 us -> 11.1 us
  matrix products: 31.6 us -> 0 us
  between operations: 14.5 us -> 1.18 us
  other arithmetic: 13.5 us -> 1.78 us
  Pallas kernels: 0 us -> 10.6 us
    unnamed x5 -> x0, waiting for transfers between devices: 245 us -> none
    all_gather x2 -> x0, waiting for transfers between devices: 237 us -> none  [the longest x1 123 us: on_device(): whole = lax.all_gather(spectrum, 'tensor', axis=0, tiled=True)]
    ppermute x0 -> x41, waiting for transfers between devices: none -> 120 us  [the longest x36 100 us: send(): return lax.ppermute(a, 'tensor', moves)]
    psum x1 -> x0, waiting for transfers between devices: 118 us -> none  [on_device(): lax.psum(in_part.astype(jnp.bfloat16), 'bulk').astype(jnp.float32)]
    ppermute x0 -> x41, starting transfers between devices: none -> 83.1 us  [the longest x36 57.8 us: send(): return lax.ppermute(a, 'tensor', moves)]
    dot_general x5 -> x0, matrix products: 31.6 us -> none  [the longest x1 8.27 us: on_device(): jnp.einsum('cr,ctk->rtk', in_factor, whole, preferred_element_type=jnp.fl...]
    convert_element_type x1 -> x0, local copies, waits for them, and re-layouts: 26.6 us -> none  [on_device(): jnp.einsum('cr,rtk->ctk', rows, pulled, preferred_element_type=jnp.float32)]
    unnamed x29 -> x24, local copies, waits for them, and re-layouts: 16.6 us -> 1.02 us
  transfers between devices with their start and end apart: 4 -> 41, of which waited for: 4 -> 22; matrix products, arithmetic and copies ran while one was open for 8% -> 4% of each run, Pallas kernels for 0% -> 0%
where the time goes in v1:
time: 232 us; the launch traced here: 228 us
  waiting for transfers between devices  120 us (52%)
  starting transfers between devices  83.1 us (36%)
  local copies, waits for them, and re-layouts  11.1 us (5%)
  Pallas kernels  10.6 us (5%)
    ppermute x36, waiting for transfers between devices, send(): return lax.ppermute(a, 'tensor', moves)  100 us
    ppermute x36, starting transfers between devices, send(): return lax.ppermute(a, 'tensor', moves)  57.8 us
    ppermute x5, starting transfers between devices, send_bulk(): return lax.ppermute(a, 'bulk', [(i, move(i)) for i in range(16)])  25.2 us
    ppermute x5, waiting for transfers between devices, send_bulk(): return lax.ppermute(a, 'bulk', [(i, move(i)) for i in range(16)])  20.1 us
    pallas_call x1, Pallas kernels, compute(): pl.pallas_call(functools.partial(body, steps), grid_spec=pltpu.PrefetchSc...  10.6 us
  transfers between devices with their start and end apart: 41, of which 22 were waited for; matrix products, arithmetic and copies ran while one was open for 4% of the time, Pallas kernels for 0%

profile of v1, /device:TPU:1, one launch (start us, length us, event | category | flops | bytes accessed | tf_op | source)
XLA Modules:
  0.0 228.1 jit_solution(1257956555354143364)
XLA Ops:
  2.4 3.4 %collective-permute-start.10 = (bf16[2,16,2560]{2,1,0:T(8,128)(2,1)S(1)}, bf16[2,16,2560]{2,1,0:T(8,128)(2,1)S(1)}, u32[]{:S(2)}, u32[]{:S(2)}) collective-permute-start(bf16[2,16,2560]{2,1,0:T(8,128)(2,1)S(1)} %bitcast.83), channel_id=1, source_target_pairs={{0,3},{1,0},{2,1},{3,2},{4,7},{5,4},{6,5},{7,6},{8,11},{9,8},{10,9... | collective-permute-start | bytes 491528 | tf_op jit(solution)/shard_map/ppermute | solution.py:32
  18.0 2.1 collective-permute-done
  25.1 9.6 %collective-permute-done.19.refs_17_ = bf16[2,64,256]{2,1,0:T(8,128)(2,1)S(1)} collective-permute-done((bf16[2,64,256]{2,1,0:T(8,128)(2,1)S(1)}, bf16[2,64,256]{2,1,0:T(8,128)(2,1)S(1)}, u32[]{:S(2)}, u32[]{:S(2)}) %collective-permute-start.19) | collective-permute-done | bytes 65568 | tf_op jit(solution)/shard_map/ppermute | solution.py:32
  35.5 2.8 %collective-permute-start.17 = (bf16[2,64,2560]{2,1,0:T(8,128)(2,1)S(1)}, bf16[2,64,2560]{2,1,0:T(8,128)(2,1)S(1)}, u32[]{:S(2)}, u32[]{:S(2)}) collective-permute-start(bf16[2,64,2560]{2,1,0:T(8,128)(2,1)S(1)} %get-tuple-element.27), channel_id=1, source_target_pairs={{0,2},{1,3},{2,0},{3,1},{4,6},{5,7},{6,4},{7,5},{8,10},{9,11},{10,... | collective-permute-start | bytes 1966088 | tf_op jit(solution)/shard_map/ppermute | solution.py:32
  44.4 2.3 collective-permute-done.17.refs_14_
  46.6 2.9 %collective-permute-start.18 = (bf16[2,64,2560]{2,1,0:T(8,128)(2,1)}, bf16[2,64,2560]{2,1,0:T(8,128)(2,1)}, u32[]{:S(2)}, u32[]{:S(2)}) collective-permute-start(bf16[2,64,2560]{2,1,0:T(8,128)(2,1)} %get-tuple-element.26), channel_id=1, source_target_pairs={{0,3},{1,0},{2,1},{3,2},{4,7},{5,4},{6,5},{7,6},{8,11},{9,8},{10,9... | collective-permute-start | bytes 1966088 | tf_op jit(solution)/shard_map/ppermute | solution.py:32
  55.7 8.7 %collective-permute-done.18.refs_15_ = bf16[2,64,2560]{2,1,0:T(8,128)(2,1)} collective-permute-done((bf16[2,64,2560]{2,1,0:T(8,128)(2,1)}, bf16[2,64,2560]{2,1,0:T(8,128)(2,1)}, u32[]{:S(2)}, u32[]{:S(2)}) %collective-permute-start.18) | collective-permute-done | bytes 655392 | tf_op jit(solution)/shard_map/ppermute | solution.py:32
  64.4 6.9 %collective-permute-done.5.refs_3_ = bf16[2,64,2560]{2,1,0:T(8,128)(2,1)} collective-permute-done((bf16[2,64,2560]{2,1,0:T(8,128)(2,1)}, bf16[2,64,2560]{2,1,0:T(8,128)(2,1)}, u32[]{:S(2)}, u32[]{:S(2)}) %collective-permute-start.5) | collective-permute-done | bytes 655392 | tf_op jit(solution)/shard_map/ppermute | solution.py:32
  71.3 19.0 %collective-permute-done.15.refs_11_ = bf16[2,64,2560]{2,1,0:T(8,128)(2,1)} collective-permute-done((bf16[2,64,2560]{2,1,0:T(8,128)(2,1)}, bf16[2,64,2560]{2,1,0:T(8,128)(2,1)}, u32[]{:S(2)}, u32[]{:S(2)}) %collective-permute-start.15) | collective-permute-done | bytes 655392 | tf_op jit(solution)/shard_map/ppermute | solution.py:32
  90.4 16.1 %collective-permute-done.7.refs_5_ = bf16[2,64,2560]{2,1,0:T(8,128)(2,1)} collective-permute-done((bf16[2,64,2560]{2,1,0:T(8,128)(2,1)}, bf16[2,64,2560]{2,1,0:T(8,128)(2,1)}, u32[]{:S(2)}, u32[]{:S(2)}) %collective-permute-start.7) | collective-permute-done | bytes 655392 | tf_op jit(solution)/shard_map/ppermute | solution.py:32
  106.5 10.6 %shard_map.93 = (bf16[2,64,2560]{2,1,0:T(8,128)(2,1)S(1)}, bf16[2,64,2560]{2,1,0:T(8,128)(2,1)S(1)}, bf16[2,64,2560]{2,1,0:T(8,128)(2,1)S(1)}, bf16[2,64,2560]{2...) custom-call(s32[17]{0:T(128)S(1)} %pad_add_fusion.info, ...), custom_call_target="tpu_custom_call" | custom-call | flops 3355443200 | bytes 26214400 | tf_op jit(solution)/shard_map/pallas_call | solution.py:115
  118.2 2.7 %collective-permute-start.34 = (f32[2,64,256]{2,1,0:T(8,128)S(1)}, f32[2,64,256]{2,1,0:T(8,128)S(1)}, u32[]{:S(2)}, u32[]{:S(2)}) collective-permute-start(f32[2,64,256]{2,1,0:T(8,128)S(1)} %get-tuple-element.44), channel_id=1, source_target_pairs={{0,2},{1,3},{2,0},{3,1},{4,6},{5,7},{6,4},{7,5},{8,10},{9,11},{10,... | collective-permute-start | bytes 393224 | tf_op jit(solution)/shard_map/ppermute | solution.py:32
  121.5 2.1 collective-permute-done.34
  123.5 2.4 %collective-permute-done.35 = f32[2,64,256]{2,1,0:T(8,128)S(1)} collective-permute-done((f32[2,64,256]{2,1,0:T(8,128)S(1)}, f32[2,64,256]{2,1,0:T(8,128)S(1)}, u32[]{:S(2)}, u32[]{:S(2)}) %collective-permute-start.35) | collective-permute-done | bytes 131104 | tf_op jit(solution)/shard_map/ppermute | solution.py:32
  125.9 13.2 %collective-permute-start.36 = (f32[2,64,256]{2,1,0:T(8,128)S(1)}, f32[2,64,256]{2,1,0:T(8,128)S(1)}, u32[]{:S(2)}, u32[]{:S(2)}) collective-permute-start(f32[2,64,256]{2,1,0:T(8,128)S(1)} %fusion.6), channel_id=1, source_target_pairs={{0,16},{16,0},{32,48},{48,32},{64,80},{80,64},{96,112},{112,96},{1... | collective-permute-start | bytes 393224 | tf_op jit(solution)/shard_map/ppermute | solution.py:36
  140.1 3.0 %collective-permute-start.37 = (f32[2,64,256]{2,1,0:T(8,128)S(1)}, f32[2,64,256]{2,1,0:T(8,128)S(1)}, u32[]{:S(2)}, u32[]{:S(2)}) collective-permute-start(f32[2,64,256]{2,1,0:T(8,128)S(1)} %add.178), channel_id=1, source_target_pairs={{0,64},{16,80},{32,96},{48,112},{64,0},{80,16},{96,32},{112,48},{1... | collective-permute-start | bytes 393224 | tf_op jit(solution)/shard_map/ppermute | solution.py:36
  143.5 2.3 collective-permute-start.39
  147.3 2.4 %collective-permute-done.38 = f32[2,64,256]{2,1,0:T(8,128)S(1)} collective-permute-done((f32[2,64,256]{2,1,0:T(8,128)S(1)}, f32[2,64,256]{2,1,0:T(8,128)S(1)}, u32[]{:S(2)}, u32[]{:S(2)}) %collective-permute-start.38) | collective-permute-done | bytes 131104 | tf_op jit(solution)/shard_map/ppermute | solution.py:36
  151.1 6.4 %collective-permute-start.40 = (f32[2,64,256]{2,1,0:T(8,128)S(1)}, f32[2,64,256]{2,1,0:T(8,128)S(1)}, u32[]{:S(2)}, u32[]{:S(2)}) collective-permute-start(f32[2,64,256]{2,1,0:T(8,128)S(1)} %add_add_fusion), channel_id=1, source_target_pairs={{0,128},{16,144},{32,160},{48,176},{64,192},{80,208},{96,224},{112... | collective-permute-start | bytes 393224 | tf_op jit(solution)/shard_map/ppermute | solution.py:36
  159.6 16.7 %collective-permute-done.40 = f32[2,64,256]{2,1,0:T(8,128)S(1)} collective-permute-done((f32[2,64,256]{2,1,0:T(8,128)S(1)}, f32[2,64,256]{2,1,0:T(8,128)S(1)}, u32[]{:S(2)}, u32[]{:S(2)}) %collective-permute-start.40) | collective-permute-done | bytes 131104 | tf_op jit(solution)/shard_map/ppermute | solution.py:36
  179.2 10.6 %collective-permute-done.24 = bf16[2,64,2560]{2,1,0:T(8,128)(2,1)S(1)} collective-permute-done((bf16[2,64,2560]{2,1,0:T(8,128)(2,1)S(1)}, bf16[2,64,2560]{2,1,0:T(8,128)(2,1)S(1)}, u32[]{:S(2)}, u32[]{:S(2)}) %collective-permute-start.24) | collective-permute-done | bytes 655392 | tf_op jit(solution)/shard_map/ppermute | solution.py:32
  192.3 15.4 %collective-permute-start.26 = (bf16[2,64,2560]{2,1,0:T(8,128)(2,1)S(1)}, bf16[2,64,2560]{2,1,0:T(8,128)(2,1)S(1)}, u32[]{:S(2)}, u32[]{:S(2)}) collective-permute-start(bf16[2,64,2560]{2,1,0:T(8,128)(2,1)S(1)} %add_convert_fusion.1), channel_id=1, source_target_pairs={{0,4},{1,5},{2,6},{3,7},{4,0},{5,1},{6,2},{7,3},{8,12},{9,13},{10,... | collective-permute-start | bytes 1966088 | tf_op jit(solution)/shard_map/ppermute | solution.py:32
  208.5 10.6 %collective-permute-done.26 = bf16[2,64,2560]{2,1,0:T(8,128)(2,1)S(1)} collective-permute-done((bf16[2,64,2560]{2,1,0:T(8,128)(2,1)S(1)}, bf16[2,64,2560]{2,1,0:T(8,128)(2,1)S(1)}, u32[]{:S(2)}, u32[]{:S(2)}) %collective-permute-start.26) | collective-permute-done | bytes 655392 | tf_op jit(solution)/shard_map/ppermute | solution.py:32
  221.5 2.2 collective-permute-done.27
  (116 shorter events, 52.6 us)
Async XLA Ops:
  8.2 11.9 %collective-permute-start = (bf16[2,16,2560]{2,1,0:T(8,128)(2,1)S(1)}, bf16[2,16,2560]{2,1,0:T(8,128)(2,1)S(1)}, u32[]{:S(2)}, u32[]{:S(2)}) collective-permute-start(bf16[2,16,2560]{2,1,0:T(8,128)(2,1)S(1)} %bitcast.79), channel_id=1, source_target_pairs={{0,1},{1,2},{2,3},{3,0},{4,5},{5,6},{6,7},{7,4},{8,9},{9,10},{10,1... | collective-permute-start | bytes 491528 | tf_op jit(solution)/shard_map/ppermute | solution.py:32
  9.9 11.6 %collective-permute-start.1 = (bf16[2,16,2560]{2,1,0:T(8,128)(2,1)S(1)}, bf16[2,16,2560]{2,1,0:T(8,128)(2,1)S(1)}, u32[]{:S(2)}, u32[]{:S(2)}) collective-permute-start(bf16[2,16,2560]{2,1,0:T(8,128)(2,1)S(1)} %bitcast.80), channel_id=1, source_target_pairs={{0,2},{1,3},{2,0},{3,1},{4,6},{5,7},{6,4},{7,5},{8,10},{9,11},{10,... | collective-permute-start | bytes 491528 | tf_op jit(solution)/shard_map/ppermute | solution.py:32
  14.5 26.9 %collective-permute-start.11 = (bf16[2,64,2560]{2,1,0:T(8,128)(2,1)S(1)}, bf16[2,64,2560]{2,1,0:T(8,128)(2,1)S(1)}, u32[]{:S(2)}, u32[]{:S(2)}) collective-permute-start(bf16[2,64,2560]{2,1,0:T(8,128)(2,1)S(1)} %pad_maximum_fusion.1.refs_6_), channel_id=1, source_target_pairs={{0,4},{1,5},{2,6},{3,7},{4,0},{5,1},{6,2},{7,3},{8,12},{9,13},{10,... | collective-permute-start | bytes 1966088 | tf_op jit(solution)/shard_map/ppermute | solution.py:32
  18.0 21.8 %collective-permute-start.16 = (bf16[2,64,2560]{2,1,0:T(8,128)(2,1)S(1)}, bf16[2,64,2560]{2,1,0:T(8,128)(2,1)S(1)}, u32[]{:S(2)}, u32[]{:S(2)}) collective-permute-start(bf16[2,64,2560]{2,1,0:T(8,128)(2,1)S(1)} %get-tuple-element.28), channel_id=1, source_target_pairs={{0,1},{1,2},{2,3},{3,0},{4,5},{5,6},{6,7},{7,4},{8,9},{9,10},{10,1... | collective-permute-start | bytes 1966088 | tf_op jit(solution)/shard_map/ppermute | solution.py:32
  21.5 21.3 %collective-permute-start.3 = (bf16[2,64,2560]{2,1,0:T(8,128)(2,1)S(1)}, bf16[2,64,2560]{2,1,0:T(8,128)(2,1)S(1)}, u32[]{:S(2)}, u32[]{:S(2)}) collective-permute-start(bf16[2,64,2560]{2,1,0:T(8,128)(2,1)S(1)} %pad_maximum_fusion.refs_0_), channel_id=1, source_target_pairs={{0,4},{1,5},{2,6},{3,7},{4,0},{5,1},{6,2},{7,3},{8,12},{9,13},{10,... | collective-permute-start | bytes 1966088 | tf_op jit(solution)/shard_map/ppermute | solution.py:32
  23.3 11.4 %collective-permute-start.19 = (bf16[2,64,256]{2,1,0:T(8,128)(2,1)S(1)}, bf16[2,64,256]{2,1,0:T(8,128)(2,1)S(1)}, u32[]{:S(2)}, u32[]{:S(2)}) collective-permute-start(bf16[2,64,256]{2,1,0:T(8,128)(2,1)S(1)} %pad_maximum_fusion.3.refs_16_), channel_id=1, source_target_pairs={{0,1},{1,2},{2,3},{3,0},{4,5},{5,6},{6,7},{7,4},{8,9},{9,10},{10,1... | collective-permute-start | bytes 196616 | tf_op jit(solution)/shard_map/ppermute | solution.py:32
  24.0 11.5 %collective-permute-start.20 = (bf16[2,64,256]{2,1,0:T(8,128)(2,1)S(1)}, bf16[2,64,256]{2,1,0:T(8,128)(2,1)S(1)}, u32[]{:S(2)}, u32[]{:S(2)}) collective-permute-start(bf16[2,64,256]{2,1,0:T(8,128)(2,1)S(1)} %pad_maximum_fusion.3.refs_16_), channel_id=1, source_target_pairs={{0,2},{1,3},{2,0},{3,1},{4,6},{5,7},{6,4},{7,5},{8,10},{9,11},{10,... | collective-permute-start | bytes 196616 | tf_op jit(solution)/shard_map/ppermute | solution.py:32
  35.5 11.1 %collective-permute-start.17 = (bf16[2,64,2560]{2,1,0:T(8,128)(2,1)S(1)}, bf16[2,64,2560]{2,1,0:T(8,128)(2,1)S(1)}, u32[]{:S(2)}, u32[]{:S(2)}) collective-permute-start(bf16[2,64,2560]{2,1,0:T(8,128)(2,1)S(1)} %get-tuple-element.27), channel_id=1, source_target_pairs={{0,2},{1,3},{2,0},{3,1},{4,6},{5,7},{6,4},{7,5},{8,10},{9,11},{10,... | collective-permute-start | bytes 1966088 | tf_op jit(solution)/shard_map/ppermute | solution.py:32
  38.3 11.2 %collective-permute-start.12 = (bf16[2,64,2560]{2,1,0:T(8,128)(2,1)S(1)}, bf16[2,64,2560]{2,1,0:T(8,128)(2,1)}, u32[]{:S(2)}, u32[]{:S(2)}) collective-permute-start(bf16[2,64,2560]{2,1,0:T(8,128)(2,1)S(1)} %pad_maximum_fusion.1.refs_6_), channel_id=1, source_target_pairs={{4,8},{5,9},{6,10},{7,11},{8,4},{9,5},{10,6},{11,7},{20,24},{21,25... | collective-permute-start | bytes 1966088 | tf_op jit(solution)/shard_map/ppermute | solution.py:32
  39.8 11.0 %collective-permute-start.4 = (bf16[2,64,2560]{2,1,0:T(8,128)(2,1)S(1)}, bf16[2,64,2560]{2,1,0:T(8,128)(2,1)}, u32[]{:S(2)}, u32[]{:S(2)}) collective-permute-start(bf16[2,64,2560]{2,1,0:T(8,128)(2,1)S(1)} %pad_maximum_fusion.refs_0_), channel_id=1, source_target_pairs={{4,8},{5,9},{6,10},{7,11},{8,4},{9,5},{10,6},{11,7},{20,24},{21,25... | collective-permute-start | bytes 1966088 | tf_op jit(solution)/shard_map/ppermute | solution.py:32
  46.6 17.8 %collective-permute-start.18 = (bf16[2,64,2560]{2,1,0:T(8,128)(2,1)}, bf16[2,64,2560]{2,1,0:T(8,128)(2,1)}, u32[]{:S(2)}, u32[]{:S(2)}) collective-permute-start(bf16[2,64,2560]{2,1,0:T(8,128)(2,1)} %get-tuple-element.26), channel_id=1, source_target_pairs={{0,3},{1,0},{2,1},{3,2},{4,7},{5,4},{6,5},{7,6},{8,11},{9,8},{10,9... | collective-permute-start | bytes 1966088 | tf_op jit(solution)/shard_map/ppermute | solution.py:32
  49.5 14.9 %collective-permute-start.13 = (bf16[2,64,2560]{2,1,0:T(8,128)(2,1)}, bf16[2,64,2560]{2,1,0:T(8,128)(2,1)}, u32[]{:S(2)}, u32[]{:S(2)}) collective-permute-start(bf16[2,64,2560]{2,1,0:T(8,128)(2,1)} %collective-permute-done.12.refs_8_), channel_id=1, source_target_pairs={{4,0},{5,1},{6,2},{7,3},{8,12},{9,13},{10,14},{11,15},{20,16},{21,... | collective-permute-start | bytes 1966088 | tf_op jit(solution)/shard_map/ppermute | solution.py:32
  50.8 20.5 %collective-permute-start.5 = (bf16[2,64,2560]{2,1,0:T(8,128)(2,1)}, bf16[2,64,2560]{2,1,0:T(8,128)(2,1)}, u32[]{:S(2)}, u32[]{:S(2)}) collective-permute-start(bf16[2,64,2560]{2,1,0:T(8,128)(2,1)} %collective-permute-done.4.refs_2_), channel_id=1, source_target_pairs={{4,0},{5,1},{6,2},{7,3},{8,12},{9,13},{10,14},{11,15},{20,16},{21,... | collective-permute-start | bytes 1966088 | tf_op jit(solution)/shard_map/ppermute | solution.py:32
  52.1 38.2 %collective-permute-start.15 = (bf16[2,64,2560]{2,1,0:T(8,128)(2,1)}, bf16[2,64,2560]{2,1,0:T(8,128)(2,1)}, u32[]{:S(2)}, u32[]{:S(2)}) collective-permute-start(bf16[2,64,2560]{2,1,0:T(8,128)(2,1)} %collective-permute-done.14.refs_10_), channel_id=1, source_target_pairs={{4,0},{5,1},{6,2},{7,3},{8,12},{9,13},{10,14},{11,15},{20,16},{21,... | collective-permute-start | bytes 1966088 | tf_op jit(solution)/shard_map/ppermute | solution.py:32
  53.5 53.1 %collective-permute-start.7 = (bf16[2,64,2560]{2,1,0:T(8,128)(2,1)}, bf16[2,64,2560]{2,1,0:T(8,128)(2,1)}, u32[]{:S(2)}, u32[]{:S(2)}) collective-permute-start(bf16[2,64,2560]{2,1,0:T(8,128)(2,1)} %collective-permute-done.6.refs_4_), channel_id=1, source_target_pairs={{4,0},{5,1},{6,2},{7,3},{8,12},{9,13},{10,14},{11,15},{20,16},{21,... | collective-permute-start | bytes 1966088 | tf_op jit(solution)/shard_map/ppermute | solution.py:32
  125.9 14.1 %collective-permute-start.36 = (f32[2,64,256]{2,1,0:T(8,128)S(1)}, f32[2,64,256]{2,1,0:T(8,128)S(1)}, u32[]{:S(2)}, u32[]{:S(2)}) collective-permute-start(f32[2,64,256]{2,1,0:T(8,128)S(1)} %fusion.6), channel_id=1, source_target_pairs={{0,16},{16,0},{32,48},{48,32},{64,80},{80,64},{96,112},{112,96},{1... | collective-permute-start | bytes 393224 | tf_op jit(solution)/shard_map/ppermute | solution.py:36
  145.8 44.8 %collective-permute-start.30 = (bf16[2,64,2560]{2,1,0:T(8,128)(2,1)S(1)}, bf16[2,64,2560]{2,1,0:T(8,128)(2,1)S(1)}, u32[]{:S(2)}, u32[]{:S(2)}) collective-permute-start(bf16[2,64,2560]{2,1,0:T(8,128)(2,1)S(1)} %get-tuple-element.21), channel_id=1, source_target_pairs={{0,3},{1,0},{2,1},{3,2},{4,7},{5,4},{6,5},{7,6},{8,11},{9,8},{10,9... | collective-permute-start | bytes 1966088 | tf_op jit(solution)/shard_map/ppermute | solution.py:32
  146.1 45.3 %collective-permute-start.31 = (bf16[2,64,2560]{2,1,0:T(8,128)(2,1)S(1)}, bf16[2,64,2560]{2,1,0:T(8,128)(2,1)S(1)}, u32[]{:S(2)}, u32[]{:S(2)}) collective-permute-start(bf16[2,64,2560]{2,1,0:T(8,128)(2,1)S(1)} %get-tuple-element.22), channel_id=1, source_target_pairs={{0,2},{1,3},{2,0},{3,1},{4,6},{5,7},{6,4},{7,5},{8,10},{9,11},{10,... | collective-permute-start | bytes 1966088 | tf_op jit(solution)/shard_map/ppermute | solution.py:32
  146.7 61.0 %collective-permute-start.32 = (bf16[2,64,2560]{2,1,0:T(8,128)(2,1)S(1)}, bf16[2,64,2560]{2,1,0:T(8,128)(2,1)S(1)}, u32[]{:S(2)}, u32[]{:S(2)}) collective-permute-start(bf16[2,64,2560]{2,1,0:T(8,128)(2,1)S(1)} %get-tuple-element.23), channel_id=1, source_target_pairs={{0,1},{1,2},{2,3},{3,0},{4,5},{5,6},{6,7},{7,4},{8,9},{9,10},{10,1... | collective-permute-start | bytes 1966088 | tf_op jit(solution)/shard_map/ppermute | solution.py:32
  149.7 28.6 %collective-permute-start.22 = (bf16[2,64,2560]{2,1,0:T(8,128)(2,1)S(1)}, bf16[2,64,2560]{2,1,0:T(8,128)(2,1)S(1)}, u32[]{:S(2)}, u32[]{:S(2)}) collective-permute-start(bf16[2,64,2560]{2,1,0:T(8,128)(2,1)S(1)} %get-tuple-element.17), channel_id=1, source_target_pairs={{0,4},{1,5},{2,6},{3,7},{12,8},{13,9},{14,10},{15,11},{16,20},{17,... | collective-permute-start | bytes 1966088 | tf_op jit(solution)/shard_map/ppermute | solution.py:32
  151.1 25.2 %collective-permute-start.40 = (f32[2,64,256]{2,1,0:T(8,128)S(1)}, f32[2,64,256]{2,1,0:T(8,128)S(1)}, u32[]{:S(2)}, u32[]{:S(2)}) collective-permute-start(f32[2,64,256]{2,1,0:T(8,128)S(1)} %add_add_fusion), channel_id=1, source_target_pairs={{0,128},{16,144},{32,160},{48,176},{64,192},{80,208},{96,224},{112... | collective-permute-start | bytes 393224 | tf_op jit(solution)/shard_map/ppermute | solution.py:36
  176.3 13.5 %collective-permute-start.24 = (bf16[2,64,2560]{2,1,0:T(8,128)(2,1)S(1)}, bf16[2,64,2560]{2,1,0:T(8,128)(2,1)S(1)}, u32[]{:S(2)}, u32[]{:S(2)}) collective-permute-start(bf16[2,64,2560]{2,1,0:T(8,128)(2,1)S(1)} %get-tuple-element.19), channel_id=1, source_target_pairs={{0,4},{1,5},{2,6},{3,7},{12,8},{13,9},{14,10},{15,11},{16,20},{17,... | collective-permute-start | bytes 1966088 | tf_op jit(solution)/shard_map/ppermute | solution.py:32
  178.5 30.0 %collective-permute-start.23 = (bf16[2,64,2560]{2,1,0:T(8,128)(2,1)S(1)}, bf16[2,64,2560]{2,1,0:T(8,128)(2,1)S(1)}, u32[]{:S(2)}, u32[]{:S(2)}) collective-permute-start(bf16[2,64,2560]{2,1,0:T(8,128)(2,1)S(1)} %add_convert_fusion.3), channel_id=1, source_target_pairs={{4,8},{5,9},{6,10},{7,11},{8,4},{9,5},{10,6},{11,7},{20,24},{21,25... | collective-permute-start | bytes 1966088 | tf_op jit(solution)/shard_map/ppermute | solution.py:32
  192.3 26.8 %collective-permute-start.26 = (bf16[2,64,2560]{2,1,0:T(8,128)(2,1)S(1)}, bf16[2,64,2560]{2,1,0:T(8,128)(2,1)S(1)}, u32[]{:S(2)}, u32[]{:S(2)}) collective-permute-start(bf16[2,64,2560]{2,1,0:T(8,128)(2,1)S(1)} %add_convert_fusion.1), channel_id=1, source_target_pairs={{0,4},{1,5},{2,6},{3,7},{4,0},{5,1},{6,2},{7,3},{8,12},{9,13},{10,... | collective-permute-start | bytes 1966088 | tf_op jit(solution)/shard_map/ppermute | solution.py:32
  (25 other events, 171.1 us)

commit v2 on v0

v2 whole, which is shorter than its diff:
```python
import functools

import jax
import jax.numpy as jnp
from jax import lax
from jax.experimental import pallas as pl
from jax.experimental.pallas import tpu as pltpu
from jax.sharding import PartitionSpec as P

BF = jnp.bfloat16
F32 = jnp.float32
NX = 4
NZ = 4
ORDER = ((0, 1, 2, 3), (1, 0, 2, 3), (2, 3, 1, 0), (3, 2, 1, 0))


def x_shift(step):
    return [(z * NX + x, z * NX + (x + step) % NX) for z in range(NZ) for x in range(NX)]


def z_moves(pairs):
    return [(a * NX + x, b * NX + x) for a, b in pairs for x in range(NX)]


SWAP = z_moves([(0, 1), (1, 0), (2, 3), (3, 2)])
MIDDLE = z_moves([(1, 2), (2, 1)])
OUTWARD = z_moves([(1, 0), (2, 3)])
INWARD = z_moves([(0, 1), (3, 2)])


def send(a, moves):
    return lax.ppermute(a, "tensor", moves)


def send_bulk(a, move):
    return lax.ppermute(a, "bulk", [(i, move(i)) for i in range(16)])


def y_shift(step):
    return lambda i: (i // 8) * 8 + ((i // 2 % 4 + step) % 4) * 2 + i % 2


def nt_dot(a, b):
    return lax.dot_general(a, b, (((1,), (1,)), ((), ())), preferred_element_type=F32)


def nn_dot(a, b):
    return jnp.dot(a, b, preferred_element_type=F32)


TILE = 512
REST_TILE = 256
SHARE = 2048


def hbm(shape, kind):
    return pltpu.HBM(shape, kind)


def load_factors(pieces, info, tmp, acc, rows, cols_in, cols_out):
    for which, row, col in ((0, rows, cols_in), (1, None, cols_out)):
        tmp[...] = jnp.concatenate(pieces(which), axis=0).astype(F32).T
        for i in range(16):
            src = pl.ds(pl.multiple_of(info[i] * 16, 16), 16)
            acc[16 * i : 16 * i + 16, :] = tmp[src, :]
        if row is not None:
            row[...] = acc[...].astype(BF)
        col[...] = acc[...].T.astype(BF)


def store_factors(info, tmp, acc, out):
    for i in range(16):
        dst = pl.ds(pl.multiple_of(info[i] * 16, 16), 16)
        tmp[dst, :] = acc[16 * i : 16 * i + 16, :]
    out(tmp[...].T)


def products(s, g, mode, rows, cols_in, cols_out, acc_in, acc_out):
    m0, m1 = [a.astype(F32) for a in mode]
    u0, u1 = [nn_dot(cols_in[...], a) for a in s]
    v0, v1 = [nn_dot(cols_out[...], a) for a in g]
    w = [(m0 * u0 - m1 * u1).astype(BF), (m0 * u1 + m1 * u0).astype(BF)]
    p = [(v0 * m0 + v1 * m1).astype(BF), (v1 * m0 - v0 * m1).astype(BF)]
    q = [(v0 * u0 + v1 * u1).astype(BF), (v1 * u0 - v0 * u1).astype(BF)]
    acc_in[...] += nt_dot(s[0], p[0]) + nt_dot(s[1], p[1])
    acc_out[...] += nt_dot(g[0], w[0]) + nt_dot(g[1], w[1])
    return q, [nn_dot(rows[...], a) for a in p]


def shared_body(steps, at_middle, info, *refs):
    own, near, c, d = refs[0:4]
    mode, fac, old = refs[4:8], refs[8:12], refs[12 : -15]
    gm, gs, d_fac = refs[-15:-11], refs[-11:-7], refs[-7]
    rows, cols_in, cols_out, tmp, acc_in, acc_out = refs[-6:]
    k = pl.program_id(0)
    mine = info[16] == at_middle

    @pl.when(mine & (k == 0))
    def _():
        load_factors(lambda which: [f[which] for f in fac], info, tmp, acc_in, rows, cols_in, cols_out)
        acc_in[...] = jnp.zeros_like(acc_in)
        acc_out[...] = jnp.zeros_like(acc_out)

    if old:

        @pl.when(jnp.logical_not(mine) & (k == 0))
        def _():
            for src, dst in zip(old, (*gm, *gs, d_fac)):
                dst[...] = src[...]

    @pl.when(mine)
    def _():
        s, g = [
            [jnp.concatenate([own[t], near[t], c[t], d[t]], axis=0) for t in (base, base + 1)]
            for base in (0, 2)
        ]
        modes = [jnp.concatenate([m[t] for m in mode], axis=0) for t in range(2)]
        q, part = products(s, g, modes, rows, cols_in, cols_out, acc_in, acc_out)
        for t in range(2):
            whole = part[t].astype(BF)
            for i in range(4):
                gm[i][t] = q[t][64 * i : 64 * i + 64, :]
                gs[i][t] = whole[64 * i : 64 * i + 64, :]

    @pl.when(mine & (k == steps - 1))
    def _():
        for which, acc in ((0, acc_in), (1, acc_out)):

            def put(a):
                d_fac[which] = a

            store_factors(info, tmp, acc, put)


def shared(info, own, near, c, d, mode, at_middle, old=()):
    modes = own.shape[2]
    steps = modes // TILE

    def tiles(rows):
        return pl.BlockSpec((rows, 64, TILE), lambda k, n: (0, 0, jnp.where(n[16] == at_middle, k, 0)))

    last = mode[0].shape[2] // 256 - 1
    fac = pl.BlockSpec((2, 64, 256), lambda k, n: (0, 0, last))
    square = pl.BlockSpec((2, 256, 256), lambda k, n: (0, 0, 0))
    outs = pl.pallas_call(
        functools.partial(shared_body, steps, at_middle),
        grid_spec=pltpu.PrefetchScalarGridSpec(
            num_scalar_prefetch=1,
            grid=(steps,),
            in_specs=[tiles(4)] * 4
            + [tiles(2)] * 4
            + [fac] * 4
            + ([pl.BlockSpec((2, 64, TILE), lambda k, n: (0, 0, 0))] * 8 + [square] if old else []),
            out_specs=[tiles(2)] * 8 + [square],
            scratch_shapes=[pltpu.VMEM((256, 256), BF)] * 3 + [pltpu.VMEM((256, 256), F32)] * 3,
        ),
        out_shape=[hbm((2, 64, modes), BF)] * 8 + [hbm((2, 256, 256), F32)],
        input_output_aliases={13 + i: i for i in range(9)} if old else {},
        compiler_params=pltpu.CompilerParams(vmem_limit_bytes=32 * 1024 * 1024),
        cost_estimate=pl.CostEstimate(
            flops=20 * 256 * 256 * modes, bytes_accessed=10 * 256 * 2 * modes * 2, transcendentals=0
        ),
    )(info, own, near, c, d, *mode, *mode, *old)
    return list(outs)


def rest_body(steps, info, *refs):
    own, near, cd, mode, fac = refs[0], refs[1], refs[2], refs[3:7], refs[7:11]
    near_mode, near_fac = refs[11], refs[12]
    gm, gm_near, gs_own, gs_near, gs_cd, d_own = refs[13:17], *refs[17:22]
    scratch = refs[22:]
    weights = scratch[0:3], scratch[3:6]
    tmp, accs = scratch[6], (scratch[7:9], scratch[9:11])
    k = pl.program_id(0)
    middle = info[16] == 1
    here = pl.ds(pl.multiple_of(k * REST_TILE, REST_TILE), REST_TILE)

    @pl.when(middle & (k == 0))
    def _():
        load_factors(lambda which: [f[which] for f in fac], info, tmp, accs[0][0], *weights[0])
        load_factors(
            lambda which: [near_fac[2 * i + which] for i in range(4)], info, tmp, accs[0][0], *weights[1]
        )
        for pair in accs:
            for acc in pair:
                acc[...] = jnp.zeros_like(acc)

    @pl.when(middle)
    def _():
        s, g = [
            [jnp.concatenate([own[t], near[t], cd[t], cd[4 + t]], axis=0) for t in (base, base + 1)]
            for base in (0, 2)
        ]
        modes = (
            [jnp.concatenate([m[t] for m in mode], axis=0) for t in range(2)],
            [jnp.concatenate([near_mode[2 * i + t] for i in range(4)], axis=0) for t in range(2)],
        )
        q, part = products(s, g, modes[0], *weights[0], *accs[0])
        q_near, part_near = products(s, g, modes[1], *weights[1], *accs[1])
        for t in range(2):
            whole = (part[t] + part_near[t]).astype(BF)
            for i in range(4):
                gm[i][t] = q[t][64 * i : 64 * i + 64, :]
                gm_near[2 * i + t, :, here] = q_near[t][64 * i : 64 * i + 64, :]
            gs_own[t] = whole[0:64, :]
            gs_near[t] = whole[64:128, :]
            gs_cd[t] = whole[128:192, :]
            gs_cd[2 + t] = whole[192:256, :]

    @pl.when(middle & (k == steps - 1))
    def _():
        for which in range(2):

            def put_own(a):
                d_own[which] = a

            def put_near(a):
                for i in range(4):
                    gm_near[2 * i + which, :, steps * REST_TILE :] = a[64 * i : 64 * i + 64, :].astype(BF)

            store_factors(info, tmp, accs[0][which], put_own)
            store_factors(info, tmp, accs[1][which], put_near)


def rest(info, own, near, cd, mode, near_pay):
    modes = own.shape[2]
    steps = modes // REST_TILE
    first = (mode[0].shape[2] - 256 - modes) // REST_TILE

    def tiles(rows, base=0):
        return pl.BlockSpec((rows, 64, REST_TILE), lambda k, n: (0, 0, base + k * n[16]))

    def fixed(rows, at):
        return pl.BlockSpec((rows, 64, 256), lambda k, n: (0, 0, at))

    square = pl.BlockSpec((2, 256, 256), lambda k, n: (0, 0, 0))
    outs = pl.pallas_call(
        functools.partial(rest_body, steps),
        grid_spec=pltpu.PrefetchScalarGridSpec(
            num_scalar_prefetch=1,
            grid=(steps,),
            in_specs=[tiles(4), tiles(4), tiles(8)]
            + [tiles(2, first)] * 4
            + [fixed(2, mode[0].shape[2] // 256 - 1)] * 4
            + [tiles(8), fixed(8, modes // 256)],
            out_specs=[tiles(2)] * 4 + [pl.BlockSpec((8, 64, modes + 256), lambda k, n: (0, 0, 0)), tiles(2), tiles(2), tiles(4), square],
            scratch_shapes=[pltpu.VMEM((256, 256), BF)] * 6 + [pltpu.VMEM((256, 256), F32)] * 5,
        ),
        out_shape=[hbm((2, 64, modes), BF)] * 4
        + [hbm((8, 64, modes + 256), BF)]
        + [hbm((n, 64, modes), BF) for n in (2, 2, 4)]
        + [hbm((2, 256, 256), F32)],
        compiler_params=pltpu.CompilerParams(vmem_limit_bytes=40 * 1024 * 1024),
        cost_estimate=pl.CostEstimate(
            flops=40 * 256 * 256 * modes, bytes_accessed=16 * 256 * 2 * modes * 2, transcendentals=0
        ),
    )(info, own, near, cd, *mode, *mode, near_pay, near_pay)
    return list(outs[0:4]), *outs[4:]


def cut(a, x, d, size):
    return lax.dynamic_slice_in_dim(a, ((x + d) % NX) * size, size, axis=2)


def add(a, b):
    return (a.astype(F32) + b.astype(F32)).astype(BF)


def together(*arrays):
    return lax.optimization_barrier(arrays)


def on_device(spectrum, out_grad, in_factor, out_factor, mode_factor):
    scale = float(mode_factor.shape[2] * lax.axis_size("bulk")) ** (-0.5)
    size = mode_factor.shape[2] // NX
    share = SHARE
    place = lax.axis_index("tensor")
    x, z = place % NX, place // NX
    order = jnp.asarray(ORDER, jnp.int32)[z]
    blocks = order[:, None] * NX + (x - jnp.arange(NX, dtype=jnp.int32)[None, :]) % NX
    middle = (z == 1) | (z == 2)
    info = jnp.concatenate([blocks.reshape(16), middle.astype(jnp.int32)[None]])
    turn = lambda a: jnp.transpose(a, (1, 0, 2))

    both = jnp.concatenate([turn(spectrum), turn(out_grad)], axis=0)
    parts = [cut(both, x, d, size) for d in range(NX)]
    parts = [parts[0]] + [send(parts[d], x_shift(d)) for d in range(1, NX)]
    own_a = jnp.concatenate([a[:, :, :share] for a in parts], axis=1)
    own_b = jnp.concatenate([a[:, :, share:] for a in parts], axis=1)

    factors = jnp.stack([in_factor.T, out_factor.T])
    turned = turn(mode_factor)
    mode = [jnp.concatenate([cut(turned, x, d, size), factors], axis=2) for d in range(NX)]

    own_a, mode = together(own_a, mode)
    near_a, c_mid = send(own_a, SWAP), send(own_a, MIDDLE)
    mode[1], mode[3] = send(mode[1], x_shift(1)), send(mode[3], x_shift(3))
    near_a, c_mid, own_b, mode = together(near_a, c_mid, own_b, mode)
    d_mid, c_end, near_b = send(near_a, MIDDLE), send(c_mid, OUTWARD), send(own_b, INWARD)
    mode[2] = send(mode[2], x_shift(2))
    d_mid, c_end, near_b, mode = together(d_mid, c_end, near_b, mode)
    d_end = send(d_mid, OUTWARD)
    near_pay = send(jnp.concatenate([a[:, :, share:] for a in mode], axis=0), INWARD)
    cd_b = send(jnp.concatenate([own_b, near_b], axis=0), MIDDLE)
    old = shared(info, own_a, near_a, c_mid, d_mid, mode, 1)
    near_pay, cd_b, d_end, old = together(near_pay, cd_b, d_end, old)

    gm_b, gm_near, gs_own, gs_near, gs_cd, d_own = rest(info, own_b, near_b, cd_b, mode, near_pay)
    gm_near, own_a = together(gm_near, own_a)
    pay = send(gm_near, OUTWARD)
    outs = shared(info, own_a, near_a, c_end, d_end, mode, 0, old)
    gm_a, (own, near, c, d), d_fac = outs[0:4], outs[4:8], outs[8]

    d, gm_a = together(d, gm_a)
    from_d = send(d, INWARD)
    gm_a[1], gm_a[3] = send(gm_a[1], x_shift(-1)), send(gm_a[3], x_shift(-3))
    from_d, pay, c, gm_a = together(from_d, pay, c, gm_a)
    from_c = send(c, INWARD)
    d = send(jnp.concatenate([add(d, from_d), gs_cd[2:4]], axis=2), MIDDLE)
    fac = d_fac.reshape(2, NX, 64, 256)
    own_fac = d_own.reshape(2, NX, 64, 256)
    gm_b = [
        jnp.where(
            middle,
            jnp.concatenate([gm_b[i], (fac[:, i] + own_fac[:, i]).astype(BF)], axis=2),
            jnp.concatenate(
                [pay[2 * i : 2 * i + 2, :, :-256], (fac[:, i] + pay[2 * i : 2 * i + 2, :, -256:]).astype(BF)], axis=2
            ),
        )
        for i in range(NX)
    ]
    gm_b = [gm_b[0]] + [send(gm_b[i], x_shift(-i)) for i in range(1, NX)]
    from_c, d, gm_b, gm_a = together(from_c, d, gm_b, gm_a)
    zero = jnp.zeros_like(gs_own)
    near = add(jnp.concatenate([near, jnp.where(middle, gs_near, zero)], axis=2), d)
    c = send(jnp.concatenate([add(c, from_c), gs_cd[0:2]], axis=2), MIDDLE)
    near = send(near, SWAP)
    gm_a[2] = send(gm_a[2], x_shift(2))
    fac = [a[:, :, -256:].astype(F32) for a in gm_b]
    total = (fac[0] + fac[1]) + (fac[2] + fac[3])
    core = lax.axis_index("bulk") % 2
    mine, other = jnp.where(core == 0, total, total[::-1])
    mine = mine + send_bulk(other, lambda i: i ^ 1)
    mine = mine + send_bulk(mine, lambda i: i ^ 4)
    mine = mine + send_bulk(mine, lambda i: i ^ 2)
    c, near, gm_a, mine = together(c, near, gm_a, mine)
    own = jnp.concatenate([own, jnp.where(middle, gs_own, zero)], axis=2).astype(F32)
    own = (own + c.astype(F32) + near.astype(F32)).astype(BF)
    own = [own[:, 16 * i : 16 * i + 16] for i in range(NX)]
    own = [own[0]] + [send(own[i], x_shift(-i)) for i in range(1, NX)]
    mine = scale * (mine + send_bulk(mine, lambda i: i ^ 8))
    other = send_bulk(mine, lambda i: i ^ 1)
    grad_in = jnp.where(core == 0, mine, other)
    grad_out = jnp.where(core == 0, other, mine)

    def join(parts):
        out = jnp.zeros(parts[0].shape[:2] + (size * NX,), BF)
        for d in range(NX):
            out = lax.dynamic_update_slice_in_dim(out, parts[d], ((x + d) % NX) * size, axis=2)
        return turn(out)

    grad_modes = join([jnp.concatenate([a, b[:, :, :-256]], axis=2) for a, b in zip(gm_a, gm_b)])
    return (join(own), grad_modes, grad_in.T, grad_out.T)


def solution(mesh):
    return jax.shard_map(
        on_device,
        mesh=mesh,
        in_specs=(
            P("tensor", None, "bulk"),
            P("tensor", None, "bulk"),
            P(None, "tensor"),
            P(None, "tensor"),
            P("tensor", None, "bulk"),
        ),
        out_specs=(
            P("tensor", None, "bulk"),
            P("tensor", None, "bulk"),
            P(None, "tensor"),
            P(None, "tensor"),
        ),
        check_vma=False,
    )
```

time: 705 us -> 192 us (0.27)
  waiting for transfers between devices: 600 us -> 75.7 us
  starting transfers between devices: 0.34 us -> 75.4 us
  matrix products: 31.6 us -> 0 us
  local copies, waits for them, and re-layouts: 43.2 us -> 14.4 us
  Pallas kernels: 0 us -> 16.9 us
  between operations: 14.5 us -> 1.56 us
    unnamed x5 -> x0, waiting for transfers between devices: 245 us -> none
    all_gather x2 -> x0, waiting for transfers between devices: 237 us -> none  [the longest x1 123 us: on_device(): whole = lax.all_gather(spectrum, 'tensor', axis=0, tiled=True)]
    psum x1 -> x0, waiting for transfers between devices: 118 us -> none  [on_device(): lax.psum(in_part.astype(jnp.bfloat16), 'bulk').astype(jnp.float32)]
    ppermute x0 -> x34, waiting for transfers between devices: none -> 75.7 us  [the longest x29 71.3 us: send(): return lax.ppermute(a, 'tensor', moves)]
    ppermute x0 -> x34, starting transfers between devices: none -> 75.4 us  [the longest x29 57.7 us: send(): return lax.ppermute(a, 'tensor', moves)]
    dot_general x5 -> x0, matrix products: 31.6 us -> none  [the longest x1 8.27 us: on_device(): jnp.einsum('cr,ctk->rtk', in_factor, whole, preferred_element_type=jnp.fl...]
    convert_element_type x1 -> x0, local copies, waits for them, and re-layouts: 26.6 us -> none  [on_device(): jnp.einsum('cr,rtk->ctk', rows, pulled, preferred_element_type=jnp.float32)]
    pallas_call x0 -> x3, Pallas kernels: none -> 16.9 us  [the longest x2 13.8 us: shared(): pl.pallas_call(functools.partial(shared_body, steps, at_middle), grid_spe...]
  transfers between devices with their start and end apart: 4 -> 34, of which waited for: 4 -> 19; matrix products, arithmetic and copies ran while one was open for 8% -> 7% of each run, Pallas kernels for 0% -> 7%
where the time goes in v2:
time: 192 us; the launch traced here: 191 us
  waiting for transfers between devices  75.7 us (39%)
  starting transfers between devices  75.4 us (39%)
  Pallas kernels  16.9 us (9%)
  local copies, waits for them, and re-layouts  14.4 us (8%)
  other arithmetic  6.93 us (4%)
    ppermute x29, waiting for transfers between devices, send(): return lax.ppermute(a, 'tensor', moves)  71.3 us
    ppermute x29, starting transfers between devices, send(): return lax.ppermute(a, 'tensor', moves)  57.7 us
    ppermute x5, starting transfers between devices, send_bulk(): return lax.ppermute(a, 'bulk', [(i, move(i)) for i in range(16)])  17.8 us
    pallas_call x2, Pallas kernels, shared(): pl.pallas_call(functools.partial(shared_body, steps, at_middle), grid_spe...  13.8 us
    ppermute x5, waiting for transfers between devices, send_bulk(): return lax.ppermute(a, 'bulk', [(i, move(i)) for i in range(16)])  4.43 us
  transfers between devices with their start and end apart: 34, of which 19 were waited for; matrix products, arithmetic and copies ran while one was open for 7% of the time, Pallas kernels for 7%

profile of v2, /device:TPU:1, one launch (start us, length us, event | category | flops | bytes accessed | tf_op | source)
XLA Modules:
  0.0 190.9 jit_solution(4410601015040476127)
XLA Ops:
  4.6 2.5 %collective-permute-start.1 = (bf16[4,16,2560]{2,1,0:T(8,128)(2,1)S(1)}, bf16[4,16,2560]{2,1,0:T(8,128)(2,1)S(1)}, u32[]{:S(2)}, u32[]{:S(2)}) collective-permute-start(bf16[4,16,2560]{2,1,0:T(8,128)(2,1)S(1)} %get-tuple-element.192), channel_id=1, source_target_pairs={{0,2},{1,3},{2,0},{3,1},{4,6},{5,7},{6,4},{7,5},{8,10},{9,11},{10,... | collective-permute-start | bytes 983048 | tf_op jit(solution)/shard_map/ppermute | solution.py:32
  12.1 9.1 %collective-permute-done.1 = bf16[4,16,2560]{2,1,0:T(8,128)(2,1)S(1)} collective-permute-done((bf16[4,16,2560]{2,1,0:T(8,128)(2,1)S(1)}, bf16[4,16,2560]{2,1,0:T(8,128)(2,1)S(1)}, u32[]{:S(2)}, u32[]{:S(2)}) %collective-permute-start.1) | collective-permute-done | bytes 327712 | tf_op jit(solution)/shard_map/ppermute | solution.py:32
  27.9 14.6 %collective-permute-done.5.refs_5_.refs_9_.refs_4_.refs_8_ = bf16[2,64,2816]{2,1,0:T(8,128)(2,1)S(1)} collective-permute-done((bf16[2,64,2816]{2,1,0:T(8,128)(2,1)S(1)}, bf16[2,64,2816]{2,1,0:T(8,128)(2,1)S(1)}, u32[]{:S(2)}, u32[]{:S(2)}) %collective-permute-start.5) | collective-permute-done | bytes 720928 | tf_op jit(solution)/shard_map/ppermute | solution.py:32
  42.5 2.6 %collective-permute-done.3.refs_1_ = bf16[4,64,2048]{2,1,0:T(8,128)(2,1)} collective-permute-done((bf16[4,64,2048]{2,1,0:T(8,128)(2,1)S(1)}, bf16[4,64,2048]{2,1,0:T(8,128)(2,1)}, u32[]{:S(2)}, u32[]{:S(2)}) %collective-permute-start.3) | collective-permute-done | bytes 1048608 | tf_op jit(solution)/shard_map/ppermute | solution.py:32
  49.9 9.2 %collective-permute-start.9 = (bf16[4,64,512]{2,1,0:T(8,128)(2,1)S(1)}, bf16[4,64,512]{2,1,0:T(8,128)(2,1)S(1)}, u32[]{:S(2)}, u32[]{:S(2)}) collective-permute-start(bf16[4,64,512]{2,1,0:T(8,128)(2,1)S(1)} %pad_maximum_fusion.10.refs_0_), channel_id=1, source_target_pairs={{0,4},{1,5},{2,6},{3,7},{12,8},{13,9},{14,10},{15,11},{16,20},{17,... | collective-permute-start | bytes 786440 | tf_op jit(solution)/shard_map/ppermute | solution.py:32
  59.1 3.3 %collective-permute-done.9.refs_1_ = bf16[4,64,512]{2,1,0:T(8,128)(2,1)S(1)} collective-permute-done((bf16[4,64,512]{2,1,0:T(8,128)(2,1)S(1)}, bf16[4,64,512]{2,1,0:T(8,128)(2,1)S(1)}, u32[]{:S(2)}, u32[]{:S(2)}) %collective-permute-start.9) | collective-permute-done | bytes 262176 | tf_op jit(solution)/shard_map/ppermute | solution.py:32
  62.4 2.7 %collective-permute-done.10.refs_6_.refs_10_.refs_5_.refs_9_ = bf16[2,64,2816]{2,1,0:T(8,128)(2,1)S(1)} collective-permute-done((bf16[2,64,2816]{2,1,0:T(8,128)(2,1)}, bf16[2,64,2816]{2,1,0:T(8,128)(2,1)S(1)}, u32[]{:S(2)}, u32[]{:S(2)}) %collective-permute-start.10) | collective-permute-done | bytes 720928 | tf_op jit(solution)/shard_map/ppermute | solution.py:32
  65.1 10.0 %collective-permute-done.8.refs_2_ = bf16[4,64,2048]{2,1,0:T(8,128)(2,1)} collective-permute-done((bf16[4,64,2048]{2,1,0:T(8,128)(2,1)}, bf16[4,64,2048]{2,1,0:T(8,128)(2,1)}, u32[]{:S(2)}, u32[]{:S(2)}) %collective-permute-start.8) | collective-permute-done | bytes 1048608 | tf_op jit(solution)/shard_map/ppermute | solution.py:32
  77.5 5.9 %collective-permute-start.11 = (bf16[8,64,768]{2,1,0:T(8,128)(2,1)}, bf16[8,64,768]{2,1,0:T(8,128)(2,1)}, u32[]{:S(2)}, u32[]{:S(2)}) collective-permute-start(bf16[8,64,768]{2,1,0:T(8,128)(2,1)} %pad_maximum_fusion.1), channel_id=1, source_target_pairs={{0,4},{1,5},{2,6},{3,7},{12,8},{13,9},{14,10},{15,11},{16,20},{17,... | collective-permute-start | bytes 2359304 | tf_op jit(solution)/shard_map/ppermute | solution.py:32
  87.9 3.1 %shard_map.93 = (bf16[2,64,2048]{2,1,0:T(8,128)(2,1)}, bf16[2,64,2048]{2,1,0:T(8,128)(2,1)}, bf16[2,64,2048]{2,1,0:T(8,128)(2,1)}, bf16[2,64,2048]{2,1,0:T(8,128...) custom-call(s32[17]{0:T(128)S(1)} %pad_add_fusion.info, ...), custom_call_target="tpu_custom_call" | custom-call | flops 2684354560 | bytes 20971520 | tf_op jit(solution)/shard_map/pallas_call | solution.py:145
  91.1 4.6 %collective-permute-done.11.refs_11_.refs_12_ = bf16[8,64,768]{2,1,0:T(8,128)(2,1)} collective-permute-done((bf16[8,64,768]{2,1,0:T(8,128)(2,1)}, bf16[8,64,768]{2,1,0:T(8,128)(2,1)}, u32[]{:S(2)}, u32[]{:S(2)}) %collective-permute-start.11) | collective-permute-done | bytes 786464 | tf_op jit(solution)/shard_map/ppermute | solution.py:32
  95.7 2.6 %collective-permute-done.13.refs_3_ = bf16[4,64,2048]{2,1,0:T(8,128)(2,1)} collective-permute-done((bf16[4,64,2048]{2,1,0:T(8,128)(2,1)}, bf16[4,64,2048]{2,1,0:T(8,128)(2,1)}, u32[]{:S(2)}, u32[]{:S(2)}) %collective-permute-start.13) | collective-permute-done | bytes 1048608 | tf_op jit(solution)/shard_map/ppermute | solution.py:32
  98.3 3.1 %shard_map.94 = (bf16[2,64,512]{2,1,0:T(8,128)(2,1)}, bf16[2,64,512]{2,1,0:T(8,128)(2,1)}, bf16[2,64,512]{2,1,0:T(8,128)(2,1)}, bf16[2,64,512]{2,1,0:T(8,128)(2,...) custom-call(s32[17]{0:T(128)S(1)} %pad_add_fusion.info, ...), custom_call_target="tpu_custom_call" | custom-call | flops 1342177280 | bytes 8388608 | tf_op jit(solution)/shard_map/pallas_call | solution.py:237
  102.9 10.6 %shard_map.95 = (bf16[2,64,2048]{2,1,0:T(8,128)(2,1)}, bf16[2,64,2048]{2,1,0:T(8,128)(2,1)}, bf16[2,64,2048]{2,1,0:T(8,128)(2,1)}, bf16[2,64,2048]{2,1,0:T(8,128...) custom-call(s32[17]{0:T(128)S(1)} %pad_add_fusion.info, ...), custom_call_target="tpu_custom_call", output_to_operand_aliasing={{0}: (13, {}), {1}: (14, {}), {2}: (15, {}), {3}: (16, {}),... | custom-call | flops 2684354560 | bytes 20971520 | tf_op jit(solution)/shard_map/pallas_call | solution.py:145
  115.0 6.3 %collective-permute-start.16 = (bf16[2,64,2048]{2,1,0:T(8,128)(2,1)}, bf16[2,64,2048]{2,1,0:T(8,128)(2,1)S(1)}, u32[]{:S(2)}, u32[]{:S(2)}) collective-permute-start(bf16[2,64,2048]{2,1,0:T(8,128)(2,1)} %get-tuple-element.146), channel_id=1, source_target_pairs={{0,3},{1,0},{2,1},{3,2},{4,7},{5,4},{6,5},{7,6},{8,11},{9,8},{10,9... | collective-permute-start | bytes 1572872 | tf_op jit(solution)/shard_map/ppermute | solution.py:32
  122.2 7.2 %collective-permute-done.16 = bf16[2,64,2048]{2,1,0:T(8,128)(2,1)S(1)} collective-permute-done((bf16[2,64,2048]{2,1,0:T(8,128)(2,1)}, bf16[2,64,2048]{2,1,0:T(8,128)(2,1)S(1)}, u32[]{:S(2)}, u32[]{:S(2)}) %collective-permute-start.16) | collective-permute-done | bytes 524320 | tf_op jit(solution)/shard_map/ppermute | solution.py:32
  129.4 3.0 %collective-permute-done.17 = bf16[2,64,2048]{2,1,0:T(8,128)(2,1)S(1)} collective-permute-done((bf16[2,64,2048]{2,1,0:T(8,128)(2,1)}, bf16[2,64,2048]{2,1,0:T(8,128)(2,1)S(1)}, u32[]{:S(2)}, u32[]{:S(2)}) %collective-permute-start.17) | collective-permute-done | bytes 524320 | tf_op jit(solution)/shard_map/ppermute | solution.py:32
  138.5 2.4 %collective-permute-start.21 = (bf16[2,64,768]{2,1,0:T(8,128)(2,1)S(1)}, bf16[2,64,768]{2,1,0:T(8,128)(2,1)S(1)}, u32[]{:S(2)}, u32[]{:S(2)}) collective-permute-start(bf16[2,64,768]{2,1,0:T(8,128)(2,1)S(1)} %maximum_select_fusion.2), channel_id=1, source_target_pairs={{0,2},{1,3},{2,0},{3,1},{4,6},{5,7},{6,4},{7,5},{8,10},{9,11},{10,... | collective-permute-start | bytes 589832 | tf_op jit(solution)/shard_map/ppermute | solution.py:32
  141.7 4.2 %collective-permute-done.21 = bf16[2,64,768]{2,1,0:T(8,128)(2,1)S(1)} collective-permute-done((bf16[2,64,768]{2,1,0:T(8,128)(2,1)S(1)}, bf16[2,64,768]{2,1,0:T(8,128)(2,1)S(1)}, u32[]{:S(2)}, u32[]{:S(2)}) %collective-permute-start.21) | collective-permute-done | bytes 196640 | tf_op jit(solution)/shard_map/ppermute | solution.py:32
  148.8 7.8 %collective-permute-start.26 = (f32[64,256]{1,0:T(8,128)S(1)}, f32[64,256]{1,0:T(8,128)S(1)}, u32[]{:S(2)}, u32[]{:S(2)}) collective-permute-start(f32[64,256]{1,0:T(8,128)S(1)} %slice_bitcast_fusion.8), channel_id=1, source_target_pairs={{0,16},{16,0},{32,48},{48,32},{64,80},{80,64},{96,112},{112,96},{1... | collective-permute-start | bytes 196616 | tf_op jit(solution)/shard_map/ppermute | solution.py:36
  158.8 3.0 %collective-permute-start.27 = (f32[64,256]{1,0:T(8,128)S(1)}, f32[64,256]{1,0:T(8,128)S(1)}, u32[]{:S(2)}, u32[]{:S(2)}) collective-permute-start(f32[64,256]{1,0:T(8,128)S(1)} %fusion.16), channel_id=1, source_target_pairs={{0,64},{16,80},{32,96},{48,112},{64,0},{80,16},{96,32},{112,48},{1... | collective-permute-start | bytes 196616 | tf_op jit(solution)/shard_map/ppermute | solution.py:36
  167.3 4.3 %collective-permute-done.25 = bf16[2,64,2048]{2,1,0:T(8,128)(2,1)S(1)} collective-permute-done((bf16[2,64,2048]{2,1,0:T(8,128)(2,1)S(1)}, bf16[2,64,2048]{2,1,0:T(8,128)(2,1)S(1)}, u32[]{:S(2)}, u32[]{:S(2)}) %collective-permute-start.25) | collective-permute-done | bytes 524320 | tf_op jit(solution)/shard_map/ppermute | solution.py:32
  171.6 3.8 %collective-permute-start.32 = (f32[64,256]{1,0:T(8,128)S(1)}, f32[64,256]{1,0:T(8,128)S(1)}, u32[]{:S(2)}, u32[]{:S(2)}) collective-permute-start(f32[64,256]{1,0:T(8,128)S(1)} %add.200), channel_id=1, source_target_pairs={{0,128},{16,144},{32,160},{48,176},{64,192},{80,208},{96,224},{112... | collective-permute-start | bytes 196616 | tf_op jit(solution)/shard_map/ppermute | solution.py:36
  175.7 3.6 %collective-permute-start.29 = (bf16[2,16,2560]{2,1,0:T(8,128)(2,1)S(1)}, bf16[2,16,2560]{2,1,0:T(8,128)(2,1)S(1)}, u32[]{:S(2)}, u32[]{:S(2)}) collective-permute-start(bf16[2,16,2560]{2,1,0:T(8,128)(2,1)S(1)} %get-tuple-element.204), channel_id=1, source_target_pairs={{0,3},{1,0},{2,1},{3,2},{4,7},{5,4},{6,5},{7,6},{8,11},{9,8},{10,9... | collective-permute-start | bytes 491528 | tf_op jit(solution)/shard_map/ppermute | solution.py:32
  (174 shorter events, 59.6 us)
Async XLA Ops:
  4.6 16.6 %collective-permute-start.1 = (bf16[4,16,2560]{2,1,0:T(8,128)(2,1)S(1)}, bf16[4,16,2560]{2,1,0:T(8,128)(2,1)S(1)}, u32[]{:S(2)}, u32[]{:S(2)}) collective-permute-start(bf16[4,16,2560]{2,1,0:T(8,128)(2,1)S(1)} %get-tuple-element.192), channel_id=1, source_target_pairs={{0,2},{1,3},{2,0},{3,1},{4,6},{5,7},{6,4},{7,5},{8,10},{9,11},{10,... | collective-permute-start | bytes 983048 | tf_op jit(solution)/shard_map/ppermute | solution.py:32
  7.1 14.2 %collective-permute-start.2 = (bf16[4,16,2560]{2,1,0:T(8,128)(2,1)S(1)}, bf16[4,16,2560]{2,1,0:T(8,128)(2,1)S(1)}, u32[]{:S(2)}, u32[]{:S(2)}) collective-permute-start(bf16[4,16,2560]{2,1,0:T(8,128)(2,1)S(1)} %get-tuple-element.193), channel_id=1, source_target_pairs={{0,3},{1,0},{2,1},{3,2},{4,7},{5,4},{6,5},{7,6},{8,11},{9,8},{10,9... | collective-permute-start | bytes 983048 | tf_op jit(solution)/shard_map/ppermute | solution.py:32
  21.4 23.7 %collective-permute-start.3 = (bf16[4,64,2048]{2,1,0:T(8,128)(2,1)S(1)}, bf16[4,64,2048]{2,1,0:T(8,128)(2,1)}, u32[]{:S(2)}, u32[]{:S(2)}) collective-permute-start(bf16[4,64,2048]{2,1,0:T(8,128)(2,1)S(1)} %pad_maximum_fusion.refs_0_), channel_id=1, source_target_pairs={{0,4},{1,5},{2,6},{3,7},{4,0},{5,1},{6,2},{7,3},{8,12},{9,13},{10,... | collective-permute-start | bytes 3145736 | tf_op jit(solution)/shard_map/ppermute | solution.py:32
  23.1 21.9 %collective-permute-start.4 = (bf16[4,64,2048]{2,1,0:T(8,128)(2,1)S(1)}, bf16[4,64,2048]{2,1,0:T(8,128)(2,1)}, u32[]{:S(2)}, u32[]{:S(2)}) collective-permute-start(bf16[4,64,2048]{2,1,0:T(8,128)(2,1)S(1)} %pad_maximum_fusion.refs_0_), channel_id=1, source_target_pairs={{4,8},{5,9},{6,10},{7,11},{8,4},{9,5},{10,6},{11,7},{20,24},{21,25... | collective-permute-start | bytes 3145736 | tf_op jit(solution)/shard_map/ppermute | solution.py:32
  24.8 17.7 %collective-permute-start.5 = (bf16[2,64,2816]{2,1,0:T(8,128)(2,1)S(1)}, bf16[2,64,2816]{2,1,0:T(8,128)(2,1)S(1)}, u32[]{:S(2)}, u32[]{:S(2)}) collective-permute-start(bf16[2,64,2816]{2,1,0:T(8,128)(2,1)S(1)} %get-tuple-element.95), channel_id=1, source_target_pairs={{0,1},{1,2},{2,3},{3,0},{4,5},{5,6},{6,7},{7,4},{8,9},{9,10},{10,1... | collective-permute-start | bytes 2162696 | tf_op jit(solution)/shard_map/ppermute | solution.py:32
  26.1 16.3 %collective-permute-start.6 = (bf16[2,64,2816]{2,1,0:T(8,128)(2,1)S(1)}, bf16[2,64,2816]{2,1,0:T(8,128)(2,1)S(1)}, u32[]{:S(2)}, u32[]{:S(2)}) collective-permute-start(bf16[2,64,2816]{2,1,0:T(8,128)(2,1)S(1)} %get-tuple-element.97), channel_id=1, source_target_pairs={{0,3},{1,0},{2,1},{3,2},{4,7},{5,4},{6,5},{7,6},{8,11},{9,8},{10,9... | collective-permute-start | bytes 2162696 | tf_op jit(solution)/shard_map/ppermute | solution.py:32
  45.1 20.1 %collective-permute-start.7 = (bf16[4,64,2048]{2,1,0:T(8,128)(2,1)}, bf16[4,64,2048]{2,1,0:T(8,128)(2,1)}, u32[]{:S(2)}, u32[]{:S(2)}) collective-permute-start(bf16[4,64,2048]{2,1,0:T(8,128)(2,1)} %collective-permute-done.3.refs_1_), channel_id=1, source_target_pairs={{4,8},{5,9},{6,10},{7,11},{8,4},{9,5},{10,6},{11,7},{20,24},{21,25... | collective-permute-start | bytes 3145736 | tf_op jit(solution)/shard_map/ppermute | solution.py:32
  46.7 28.5 %collective-permute-start.8 = (bf16[4,64,2048]{2,1,0:T(8,128)(2,1)}, bf16[4,64,2048]{2,1,0:T(8,128)(2,1)}, u32[]{:S(2)}, u32[]{:S(2)}) collective-permute-start(bf16[4,64,2048]{2,1,0:T(8,128)(2,1)} %collective-permute-done.4.refs_2_), channel_id=1, source_target_pairs={{4,0},{5,1},{6,2},{7,3},{8,12},{9,13},{10,14},{11,15},{20,16},{21,... | collective-permute-start | bytes 3145736 | tf_op jit(solution)/shard_map/ppermute | solution.py:32
  48.0 17.1 %collective-permute-start.10 = (bf16[2,64,2816]{2,1,0:T(8,128)(2,1)}, bf16[2,64,2816]{2,1,0:T(8,128)(2,1)S(1)}, u32[]{:S(2)}, u32[]{:S(2)}) collective-permute-start(bf16[2,64,2816]{2,1,0:T(8,128)(2,1)} %get-tuple-element.103), channel_id=1, source_target_pairs={{0,2},{1,3},{2,0},{3,1},{4,6},{5,7},{6,4},{7,5},{8,10},{9,11},{10,... | collective-permute-start | bytes 2162696 | tf_op jit(solution)/shard_map/ppermute | solution.py:32
  49.9 12.5 %collective-permute-start.9 = (bf16[4,64,512]{2,1,0:T(8,128)(2,1)S(1)}, bf16[4,64,512]{2,1,0:T(8,128)(2,1)S(1)}, u32[]{:S(2)}, u32[]{:S(2)}) collective-permute-start(bf16[4,64,512]{2,1,0:T(8,128)(2,1)S(1)} %pad_maximum_fusion.10.refs_0_), channel_id=1, source_target_pairs={{0,4},{1,5},{2,6},{3,7},{12,8},{13,9},{14,10},{15,11},{16,20},{17,... | collective-permute-start | bytes 786440 | tf_op jit(solution)/shard_map/ppermute | solution.py:32
  75.2 23.2 %collective-permute-start.13 = (bf16[4,64,2048]{2,1,0:T(8,128)(2,1)}, bf16[4,64,2048]{2,1,0:T(8,128)(2,1)}, u32[]{:S(2)}, u32[]{:S(2)}) collective-permute-start(bf16[4,64,2048]{2,1,0:T(8,128)(2,1)} %collective-permute-done.7.refs_3_), channel_id=1, source_target_pairs={{4,0},{5,1},{6,2},{7,3},{8,12},{9,13},{10,14},{11,15},{20,16},{21,... | collective-permute-start | bytes 3145736 | tf_op jit(solution)/shard_map/ppermute | solution.py:32
  77.5 18.2 %collective-permute-start.11 = (bf16[8,64,768]{2,1,0:T(8,128)(2,1)}, bf16[8,64,768]{2,1,0:T(8,128)(2,1)}, u32[]{:S(2)}, u32[]{:S(2)}) collective-permute-start(bf16[8,64,768]{2,1,0:T(8,128)(2,1)} %pad_maximum_fusion.1), channel_id=1, source_target_pairs={{0,4},{1,5},{2,6},{3,7},{12,8},{13,9},{14,10},{15,11},{16,20},{17,... | collective-permute-start | bytes 2359304 | tf_op jit(solution)/shard_map/ppermute | solution.py:32
  101.5 30.9 %collective-permute-start.15 = (bf16[8,64,768]{2,1,0:T(8,128)(2,1)}, bf16[8,64,768]{2,1,0:T(8,128)(2,1)}, u32[]{:S(2)}, u32[]{:S(2)}) collective-permute-start(bf16[8,64,768]{2,1,0:T(8,128)(2,1)} %get-tuple-element.143), channel_id=1, source_target_pairs={{4,0},{5,1},{6,2},{7,3},{8,12},{9,13},{10,14},{11,15},{20,16},{21,... | collective-permute-start | bytes 2359304 | tf_op jit(solution)/shard_map/ppermute | solution.py:32
  115.0 14.4 %collective-permute-start.16 = (bf16[2,64,2048]{2,1,0:T(8,128)(2,1)}, bf16[2,64,2048]{2,1,0:T(8,128)(2,1)S(1)}, u32[]{:S(2)}, u32[]{:S(2)}) collective-permute-start(bf16[2,64,2048]{2,1,0:T(8,128)(2,1)} %get-tuple-element.146), channel_id=1, source_target_pairs={{0,3},{1,0},{2,1},{3,2},{4,7},{5,4},{6,5},{7,6},{8,11},{9,8},{10,9... | collective-permute-start | bytes 1572872 | tf_op jit(solution)/shard_map/ppermute | solution.py:32
  121.3 11.1 %collective-permute-start.17 = (bf16[2,64,2048]{2,1,0:T(8,128)(2,1)}, bf16[2,64,2048]{2,1,0:T(8,128)(2,1)S(1)}, u32[]{:S(2)}, u32[]{:S(2)}) collective-permute-start(bf16[2,64,2048]{2,1,0:T(8,128)(2,1)} %get-tuple-element.148), channel_id=1, source_target_pairs={{0,1},{1,2},{2,3},{3,0},{4,5},{5,6},{6,7},{7,4},{8,9},{9,10},{10,1... | collective-permute-start | bytes 1572872 | tf_op jit(solution)/shard_map/ppermute | solution.py:32
  133.8 13.4 %collective-permute-start.19 = (bf16[2,64,2560]{2,1,0:T(8,128)(2,1)S(1)}, bf16[2,64,2560]{2,1,0:T(8,128)(2,1)S(1)}, u32[]{:S(2)}, u32[]{:S(2)}) collective-permute-start(bf16[2,64,2560]{2,1,0:T(8,128)(2,1)S(1)} %pad_maximum_fusion.3), channel_id=1, source_target_pairs={{4,8},{5,9},{6,10},{7,11},{8,4},{9,5},{10,6},{11,7},{20,24},{21,25... | collective-permute-start | bytes 1966088 | tf_op jit(solution)/shard_map/ppermute | solution.py:32
  136.0 11.1 %collective-permute-start.18 = (bf16[2,64,2048]{2,1,0:T(8,128)(2,1)S(1)}, bf16[2,64,2048]{2,1,0:T(8,128)(2,1)S(1)}, u32[]{:S(2)}, u32[]{:S(2)}) collective-permute-start(bf16[2,64,2048]{2,1,0:T(8,128)(2,1)S(1)} %copy-done.6), channel_id=1, source_target_pairs={{0,4},{1,5},{2,6},{3,7},{12,8},{13,9},{14,10},{15,11},{16,20},{17,... | collective-permute-start | bytes 1572872 | tf_op jit(solution)/shard_map/ppermute | solution.py:32
  147.4 24.2 %collective-permute-start.24 = (bf16[2,64,2560]{2,1,0:T(8,128)(2,1)S(1)}, bf16[2,64,2560]{2,1,0:T(8,128)(2,1)S(1)}, u32[]{:S(2)}, u32[]{:S(2)}) collective-permute-start(bf16[2,64,2560]{2,1,0:T(8,128)(2,1)S(1)} %add_convert_fusion.1), channel_id=1, source_target_pairs={{0,4},{1,5},{2,6},{3,7},{4,0},{5,1},{6,2},{7,3},{8,12},{9,13},{10,... | collective-permute-start | bytes 1966088 | tf_op jit(solution)/shard_map/ppermute | solution.py:32
  147.9 23.7 %collective-permute-start.23 = (bf16[2,64,2560]{2,1,0:T(8,128)(2,1)S(1)}, bf16[2,64,2560]{2,1,0:T(8,128)(2,1)S(1)}, u32[]{:S(2)}, u32[]{:S(2)}) collective-permute-start(bf16[2,64,2560]{2,1,0:T(8,128)(2,1)S(1)} %pad_maximum_fusion.4), channel_id=1, source_target_pairs={{4,8},{5,9},{6,10},{7,11},{8,4},{9,5},{10,6},{11,7},{20,24},{21,25... | collective-permute-start | bytes 1966088 | tf_op jit(solution)/shard_map/ppermute | solution.py:32
  148.8 9.9 %collective-permute-start.26 = (f32[64,256]{1,0:T(8,128)S(1)}, f32[64,256]{1,0:T(8,128)S(1)}, u32[]{:S(2)}, u32[]{:S(2)}) collective-permute-start(f32[64,256]{1,0:T(8,128)S(1)} %slice_bitcast_fusion.8), channel_id=1, source_target_pairs={{0,16},{16,0},{32,48},{48,32},{64,80},{80,64},{96,112},{112,96},{1... | collective-permute-start | bytes 196616 | tf_op jit(solution)/shard_map/ppermute | solution.py:36
  156.6 15.0 %collective-permute-start.25 = (bf16[2,64,2048]{2,1,0:T(8,128)(2,1)S(1)}, bf16[2,64,2048]{2,1,0:T(8,128)(2,1)S(1)}, u32[]{:S(2)}, u32[]{:S(2)}) collective-permute-start(bf16[2,64,2048]{2,1,0:T(8,128)(2,1)S(1)} %copy-done.14), channel_id=1, source_target_pairs={{0,2},{1,3},{2,0},{3,1},{4,6},{5,7},{6,4},{7,5},{8,10},{9,11},{10,... | collective-permute-start | bytes 1572872 | tf_op jit(solution)/shard_map/ppermute | solution.py:32
  171.6 14.0 %collective-permute-start.32 = (f32[64,256]{1,0:T(8,128)S(1)}, f32[64,256]{1,0:T(8,128)S(1)}, u32[]{:S(2)}, u32[]{:S(2)}) collective-permute-start(f32[64,256]{1,0:T(8,128)S(1)} %add.200), channel_id=1, source_target_pairs={{0,128},{16,144},{32,160},{48,176},{64,192},{80,208},{96,224},{112... | collective-permute-start | bytes 196616 | tf_op jit(solution)/shard_map/ppermute | solution.py:36
  175.7 13.2 %collective-permute-start.29 = (bf16[2,16,2560]{2,1,0:T(8,128)(2,1)S(1)}, bf16[2,16,2560]{2,1,0:T(8,128)(2,1)S(1)}, u32[]{:S(2)}, u32[]{:S(2)}) collective-permute-start(bf16[2,16,2560]{2,1,0:T(8,128)(2,1)S(1)} %get-tuple-element.204), channel_id=1, source_target_pairs={{0,3},{1,0},{2,1},{3,2},{4,7},{5,4},{6,5},{7,6},{8,11},{9,8},{10,9... | collective-permute-start | bytes 491528 | tf_op jit(solution)/shard_map/ppermute | solution.py:32
  179.4 10.5 %collective-permute-start.31 = (bf16[2,16,2560]{2,1,0:T(8,128)(2,1)S(1)}, bf16[2,16,2560]{2,1,0:T(8,128)(2,1)S(1)}, u32[]{:S(2)}, u32[]{:S(2)}) collective-permute-start(bf16[2,16,2560]{2,1,0:T(8,128)(2,1)S(1)} %get-tuple-element.202), channel_id=1, source_target_pairs={{0,1},{1,2},{2,3},{3,0},{4,5},{5,6},{6,7},{7,4},{8,9},{9,10},{10,1... | collective-permute-start | bytes 491528 | tf_op jit(solution)/shard_map/ppermute | solution.py:32
  (41 other events, 338.2 us)

commit v3 on v2

v3 whole, which is shorter than its diff:
```python
import functools

import jax
import jax.numpy as jnp
from jax import lax
from jax.experimental import pallas as pl
from jax.experimental.pallas import tpu as pltpu
from jax.sharding import PartitionSpec as P

BF = jnp.bfloat16
F32 = jnp.float32
NX = 4
NZ = 4
ORDER = ((0, 1, 2, 3), (1, 0, 2, 3), (2, 3, 1, 0), (3, 2, 1, 0))


def x_shift(step):
    return [(z * NX + x, z * NX + (x + step) % NX) for z in range(NZ) for x in range(NX)]


def z_moves(pairs):
    return [(a * NX + x, b * NX + x) for a, b in pairs for x in range(NX)]


SWAP = z_moves([(0, 1), (1, 0), (2, 3), (3, 2)])
MIDDLE = z_moves([(1, 2), (2, 1)])
OUTWARD = z_moves([(1, 0), (2, 3)])
INWARD = z_moves([(0, 1), (3, 2)])


def send(a, moves):
    return lax.ppermute(a, "tensor", moves)


def send_bulk(a, move):
    return lax.ppermute(a, "bulk", [(i, move(i)) for i in range(16)])


def y_shift(step):
    return lambda i: (i // 8) * 8 + ((i // 2 % 4 + step) % 4) * 2 + i % 2


def nt_dot(a, b):
    return lax.dot_general(a, b, (((1,), (1,)), ((), ())), preferred_element_type=F32)


def nn_dot(a, b):
    return jnp.dot(a, b, preferred_element_type=F32)


TILE = 256
SHARE = 1792


def hbm(shape, kind):
    return pltpu.HBM(shape, kind)


def load_factors(pieces, info, tmp, acc, rows, cols_in, cols_out):
    for which, row, col in ((0, rows, cols_in), (1, None, cols_out)):
        tmp[...] = jnp.concatenate(pieces(which), axis=0).astype(F32).T
        for i in range(16):
            src = pl.ds(pl.multiple_of(info[i] * 16, 16), 16)
            acc[16 * i : 16 * i + 16, :] = tmp[src, :]
        if row is not None:
            row[...] = acc[...].astype(BF)
        col[...] = acc[...].T.astype(BF)


def store_factors(info, tmp, acc, out):
    for i in range(16):
        dst = pl.ds(pl.multiple_of(info[i] * 16, 16), 16)
        tmp[dst, :] = acc[16 * i : 16 * i + 16, :]
    out(tmp[...].T)


def products(s, g, mode, rows, cols_in, cols_out, acc_in, acc_out):
    m0, m1 = [a.astype(F32) for a in mode]
    u0, u1 = [nn_dot(cols_in[...], a) for a in s]
    v0, v1 = [nn_dot(cols_out[...], a) for a in g]
    w = [(m0 * u0 - m1 * u1).astype(BF), (m0 * u1 + m1 * u0).astype(BF)]
    p = [(v0 * m0 + v1 * m1).astype(BF), (v1 * m0 - v0 * m1).astype(BF)]
    q = [(v0 * u0 + v1 * u1).astype(BF), (v1 * u0 - v0 * u1).astype(BF)]
    acc_in[...] += nt_dot(s[0], p[0]) + nt_dot(s[1], p[1])
    acc_out[...] += nt_dot(g[0], w[0]) + nt_dot(g[1], w[1])
    return q, [nn_dot(rows[...], a) for a in p]


def share_step(own, near, c, d, mode, weights, accs, gm, gs):
    s, g = [
        [jnp.concatenate([own[t], near[t], c[t], d[t]], axis=0) for t in (base, base + 1)]
        for base in (0, 2)
    ]
    modes = [jnp.concatenate([m[t] for m in mode], axis=0) for t in range(2)]
    q, part = products(s, g, modes, *weights, *accs)
    for t in range(2):
        whole = part[t].astype(BF)
        for i in range(4):
            gm[i][t] = q[t][64 * i : 64 * i + 64, :]
            gs[i][t] = whole[64 * i : 64 * i + 64, :]


def shared_body(steps, info, *refs):
    own, near, c, d = refs[0:4]
    mode, fac = refs[4:8], refs[8:12]
    gm, gs, d_fac = refs[12:16], refs[16:20], refs[20]
    weights, tmp, accs = refs[21:24], refs[24], refs[25:27]
    k = pl.program_id(0)
    middle = info[16] == 1

    @pl.when(middle & (k == 0))
    def _():
        load_factors(lambda which: [f[which] for f in fac], info, tmp, accs[0], *weights)
        for acc in accs:
            acc[...] = jnp.zeros_like(acc)

    @pl.when(middle)
    def _():
        share_step(own, near, c, d, mode, weights, accs, gm, gs)

    @pl.when(middle & (k == steps - 1))
    def _():
        for which, acc in enumerate(accs):

            def put(a):
                d_fac[which] = a

            store_factors(info, tmp, acc, put)


def shared_middle(info, own, near, c, d, mode):
    modes = own.shape[2]
    steps = modes // TILE

    def tiles(rows):
        return pl.BlockSpec((rows, 64, TILE), lambda k, n: (0, 0, k * n[16]))

    last = mode[0].shape[2] // 256 - 1
    fac = pl.BlockSpec((2, 64, 256), lambda k, n: (0, 0, last))
    square = pl.BlockSpec((2, 256, 256), lambda k, n: (0, 0, 0))
    return pl.pallas_call(
        functools.partial(shared_body, steps),
        grid_spec=pltpu.PrefetchScalarGridSpec(
            num_scalar_prefetch=1,
            grid=(steps,),
            in_specs=[tiles(4)] * 4 + [tiles(2)] * 4 + [fac] * 4,
            out_specs=[tiles(2)] * 8 + [square],
            scratch_shapes=[pltpu.VMEM((256, 256), BF)] * 3 + [pltpu.VMEM((256, 256), F32)] * 3,
        ),
        out_shape=[hbm((2, 64, modes), BF)] * 8 + [hbm((2, 256, 256), F32)],
        compiler_params=pltpu.CompilerParams(vmem_limit_bytes=32 * 1024 * 1024),
        cost_estimate=pl.CostEstimate(
            flops=20 * 256 * 256 * modes, bytes_accessed=10 * 256 * 2 * modes * 2, transcendentals=0
        ),
    )(info, own, near, c, d, *mode, *mode)


def last_body(steps, info, *refs):
    own, near, c, d = refs[0:4]
    mode, fac, old = refs[4:8], refs[8:12], refs[12:20]
    own_b, near_b, cd, near_mode, near_fac = refs[20:25]
    gm, gs, d_fac = refs[25:29], refs[29:33], refs[33]
    gm_b, pay, gs_own, gs_near, gs_cd = refs[34:38], *refs[38:42]
    weights, near_weights, tmp = refs[42:45], refs[45:48], refs[48]
    accs, near_accs = refs[49:51], refs[51:53]
    k = pl.program_id(0)
    middle = info[16] == 1
    rest = pay.shape[2] - 256

    @pl.when(k == 0)
    def _():
        load_factors(lambda which: [f[which] for f in fac], info, tmp, accs[0], *weights)
        for acc in accs:
            acc[...] = jnp.zeros_like(acc)

    @pl.when(middle & (k == 0))
    def _():
        load_factors(
            lambda which: [near_fac[2 * i + which] for i in range(4)], info, tmp, near_accs[0], *near_weights
        )
        for acc in near_accs:
            acc[...] = jnp.zeros_like(acc)
        for src, dst in zip(old, (*gm, *gs)):
            dst[...] = src[...]

    @pl.when(jnp.logical_not(middle))
    def _():
        share_step(own, near, c, d, mode, weights, accs, gm, gs)

    @pl.when(middle & (k < rest // TILE))
    def _():
        s, g = [
            [jnp.concatenate([own_b[t], near_b[t], cd[t], cd[4 + t]], axis=0) for t in (base, base + 1)]
            for base in (0, 2)
        ]
        modes = [jnp.concatenate([m[t] for m in mode], axis=0) for t in range(2)]
        near_modes = [jnp.concatenate([near_mode[2 * i + t] for i in range(4)], axis=0) for t in range(2)]
        q, part = products(s, g, modes, *weights, *accs)
        q_near, part_near = products(s, g, near_modes, *near_weights, *near_accs)
        here = pl.ds(pl.multiple_of(k * TILE, TILE), TILE)
        for t in range(2):
            whole = (part[t] + part_near[t]).astype(BF)
            for i in range(4):
                gm_b[i][t] = q[t][64 * i : 64 * i + 64, :]
                pay[2 * i + t, :, here] = q_near[t][64 * i : 64 * i + 64, :]
            gs_own[t] = whole[0:64, :]
            gs_near[t] = whole[64:128, :]
            gs_cd[t] = whole[128:192, :]
            gs_cd[2 + t] = whole[192:256, :]

    @pl.when(middle & (k == rest // TILE - 1))
    def _():
        for which, acc in enumerate(near_accs):

            def put(a):
                for i in range(4):
                    pay[2 * i + which, :, rest:] = a[64 * i : 64 * i + 64, :].astype(BF)

            store_factors(info, tmp, acc, put)

    @pl.when(k == steps - 1)
    def _():
        for which, acc in enumerate(accs):

            def put(a):
                d_fac[which] = a

            store_factors(info, tmp, acc, put)


def last(info, own, near, c, d, mode, old, own_b, near_b, cd, near_pay):
    modes, rest = own.shape[2], own_b.shape[2]
    steps, rest_steps = modes // TILE, rest // TILE

    def ends(rows):
        return pl.BlockSpec((rows, 64, TILE), lambda k, n: (0, 0, k * (1 - n[16])))

    def middles(rows):
        return pl.BlockSpec((rows, 64, TILE), lambda k, n: (0, 0, jnp.minimum(k, rest_steps - 1) * n[16]))

    def fixed(rows, at):
        return pl.BlockSpec((rows, 64, 256), lambda k, n: (0, 0, at))

    both = pl.BlockSpec(
        (2, 64, TILE),
        lambda k, n: (0, 0, jnp.where(n[16] == 1, steps + jnp.minimum(k, rest_steps - 1), k)),
    )
    square = pl.BlockSpec((2, 256, 256), lambda k, n: (0, 0, 0))
    outs = pl.pallas_call(
        functools.partial(last_body, steps),
        grid_spec=pltpu.PrefetchScalarGridSpec(
            num_scalar_prefetch=1,
            grid=(steps,),
            in_specs=[ends(4)] * 4
            + [both] * 4
            + [fixed(2, mode[0].shape[2] // 256 - 1)] * 4
            + [fixed(2, 0)] * 8
            + [middles(4), middles(4), middles(8), middles(8), fixed(8, rest // 256)],
            out_specs=[ends(2)] * 8
            + [square]
            + [middles(2)] * 4
            + [pl.BlockSpec((8, 64, rest + 256), lambda k, n: (0, 0, 0))]
            + [middles(2), middles(2), middles(4)],
            scratch_shapes=[pltpu.VMEM((256, 256), BF)] * 6 + [pltpu.VMEM((256, 256), F32)] * 5,
        ),
        out_shape=[hbm((2, 64, modes), BF)] * 8
        + [hbm((2, 256, 256), F32)]
        + [hbm((2, 64, rest), BF)] * 4
        + [hbm((8, 64, rest + 256), BF)]
        + [hbm((n, 64, rest), BF) for n in (2, 2, 4)],
        input_output_aliases={13 + i: i for i in range(8)},
        compiler_params=pltpu.CompilerParams(vmem_limit_bytes=40 * 1024 * 1024),
        cost_estimate=pl.CostEstimate(
            flops=20 * 256 * 256 * modes, bytes_accessed=10 * 256 * 2 * modes * 2, transcendentals=0
        ),
    )(info, own, near, c, d, *mode, *mode, *old, own_b, near_b, cd, near_pay, near_pay)
    return list(outs[0:4]), outs[4:8], outs[8], list(outs[9:13]), *outs[13:]


def cut(a, x, d, size):
    return lax.dynamic_slice_in_dim(a, ((x + d) % NX) * size, size, axis=2)


def add(a, b):
    return (a.astype(F32) + b.astype(F32)).astype(BF)


def together(*arrays):
    return lax.optimization_barrier(arrays)


def on_device(spectrum, out_grad, in_factor, out_factor, mode_factor):
    scale = float(mode_factor.shape[2] * lax.axis_size("bulk")) ** (-0.5)
    size = mode_factor.shape[2] // NX
    share = SHARE
    place = lax.axis_index("tensor")
    x, z = place % NX, place // NX
    order = jnp.asarray(ORDER, jnp.int32)[z]
    blocks = order[:, None] * NX + (x - jnp.arange(NX, dtype=jnp.int32)[None, :]) % NX
    middle = (z == 1) | (z == 2)
    info = jnp.concatenate([blocks.reshape(16), middle.astype(jnp.int32)[None]])
    turn = lambda a: jnp.transpose(a, (1, 0, 2))

    both = jnp.concatenate([turn(spectrum), turn(out_grad)], axis=0)
    parts = [cut(both, x, d, size) for d in range(NX)]
    parts = [parts[0]] + [send(parts[d], x_shift(d)) for d in range(1, NX)]
    own_a = jnp.concatenate([a[:, :, :share] for a in parts], axis=1)
    own_b = jnp.concatenate([a[:, :, share:] for a in parts], axis=1)

    factors = jnp.stack([in_factor.T, out_factor.T])
    turned = turn(mode_factor)
    mode = [jnp.concatenate([cut(turned, x, d, size), factors], axis=2) for d in range(NX)]

    own_a, mode = together(own_a, mode)
    near_a, c_mid = send(own_a, SWAP), send(own_a, MIDDLE)
    mode = [mode[0]] + [send(mode[i], x_shift(i)) for i in range(1, NX)]
    near_a, c_mid, own_b = together(near_a, c_mid, own_b)
    d_mid, c_end, near_b = send(near_a, MIDDLE), send(c_mid, OUTWARD), send(own_b, INWARD)
    d_mid, c_end, near_b = together(d_mid, c_end, near_b)
    d_end = send(d_mid, OUTWARD)
    near_pay = send(jnp.concatenate([a[:, :, share:] for a in mode], axis=0), INWARD)
    cd_b = send(jnp.concatenate([own_b, near_b], axis=0), MIDDLE)
    *old, d_mid_fac = shared_middle(info, own_a, near_a, c_mid, d_mid, mode)
    near_pay, cd_b, d_end, old, d_mid_fac = together(near_pay, cd_b, d_end, old, d_mid_fac)
    gm_a, (own, near, c, d), d_fac, gm_b, pay, gs_own, gs_near, gs_cd = last(
        info, own_a, near_a, c_end, d_end, mode, old, own_b, near_b, cd_b, near_pay
    )

    from_d = send(d, INWARD)
    pay = send(pay, OUTWARD)
    gm_a[1], gm_a[3] = send(gm_a[1], x_shift(-1)), send(gm_a[3], x_shift(-3))
    from_d, c = together(from_d, c)
    from_c = send(c, INWARD)
    d = send(jnp.concatenate([add(d, from_d), gs_cd[2:4]], axis=2), MIDDLE)
    fac = d_fac.reshape(2, NX, 64, 256)
    mid_fac = d_mid_fac.reshape(2, NX, 64, 256)
    gm_b = [
        jnp.where(
            middle,
            jnp.concatenate([gm_b[i], (fac[:, i] + mid_fac[:, i]).astype(BF)], axis=2),
            jnp.concatenate(
                [pay[2 * i : 2 * i + 2, :, :-256], (fac[:, i] + pay[2 * i : 2 * i + 2, :, -256:]).astype(BF)], axis=2
            ),
        )
        for i in range(NX)
    ]
    gm_b = [gm_b[0]] + [send(gm_b[i], x_shift(-i)) for i in range(1, NX)]
    from_c, d, gm_a = together(from_c, d, gm_a)
    zero = jnp.zeros_like(gs_own)
    near = add(jnp.concatenate([near, jnp.where(middle, gs_near, zero)], axis=2), d)
    c = send(jnp.concatenate([add(c, from_c), gs_cd[0:2]], axis=2), MIDDLE)
    near = send(near, SWAP)
    gm_a[2] = send(gm_a[2], x_shift(2))
    fac = [a[:, :, -256:].astype(F32) for a in gm_b]
    total = (fac[0] + fac[1]) + (fac[2] + fac[3])
    core = lax.axis_index("bulk") % 2
    mine, other = jnp.where(core == 0, total, total[::-1])
    mine = mine + send_bulk(other, lambda i: i ^ 1)
    mine = mine + send_bulk(mine, lambda i: i ^ 4)
    mine = mine + send_bulk(mine, lambda i: i ^ 2)
    mine = mine + send_bulk(mine, lambda i: i ^ 8)
    c, near, gm_a, gm_b, mine = together(c, near, gm_a, gm_b, mine)
    own = jnp.concatenate([own, jnp.where(middle, gs_own, zero)], axis=2).astype(F32)
    own = (own + c.astype(F32) + near.astype(F32)).astype(BF)
    own = [own[:, 16 * i : 16 * i + 16] for i in range(NX)]
    own = [own[0]] + [send(own[i], x_shift(-i)) for i in range(1, NX)]
    mine = scale * mine
    other = send_bulk(mine, lambda i: i ^ 1)
    grad_in = jnp.where(core == 0, mine, other)
    grad_out = jnp.where(core == 0, other, mine)

    def join(parts):
        out = jnp.zeros(parts[0].shape[:2] + (size * NX,), BF)
        for d in range(NX):
            out = lax.dynamic_update_slice_in_dim(out, parts[d], ((x + d) % NX) * size, axis=2)
        return turn(out)

    grad_modes = join([jnp.concatenate([a, b[:, :, :-256]], axis=2) for a, b in zip(gm_a, gm_b)])
    return (join(own), grad_modes, grad_in.T, grad_out.T)


def solution(mesh):
    return jax.shard_map(
        on_device,
        mesh=mesh,
        in_specs=(
            P("tensor", None, "bulk"),
            P("tensor", None, "bulk"),
            P(None, "tensor"),
            P(None, "tensor"),
            P("tensor", None, "bulk"),
        ),
        out_specs=(
            P("tensor", None, "bulk"),
            P("tensor", None, "bulk"),
            P(None, "tensor"),
            P(None, "tensor"),
        ),
        check_vma=False,
    )
```

time: 192 us -> 183 us (0.953)
  waiting for transfers between devices: 75.7 us -> 57.8 us
  starting transfers between devices: 75.4 us -> 82.8 us
  local copies, waits for them, and re-layouts: 14.4 us -> 18.1 us
    ppermute x29, waiting for transfers between devices: 71.3 us -> 50.7 us  [send(): return lax.ppermute(a, 'tensor', moves)]
    ppermute x29, starting transfers between devices: 57.7 us -> 65.1 us  [send(): return lax.ppermute(a, 'tensor', moves)]
    unnamed x54 -> x68, local copies, waits for them, and re-layouts: 3.71 us -> 6.69 us
    ppermute x5, waiting for transfers between devices: 4.43 us -> 7.04 us  [send_bulk(): return lax.ppermute(a, 'bulk', [(i, move(i)) for i in range(16)])]
    pallas_call x3 -> x2, Pallas kernels: 16.9 us -> 16.1 us  [the longest x1 12.7 us: last(): pl.pallas_call(functools.partial(last_body, steps), grid_spec=pltpu.Prefe...]
  transfers between devices with their start and end apart: 34 -> 34, of which waited for: 19 -> 14; matrix products, arithmetic and copies ran while one was open for 7% -> 8% of each run, Pallas kernels for 7% -> 2%
where the time goes in v3:
time: 183 us; the launch traced here: 182 us
  starting transfers between devices  82.8 us (45%)
  waiting for transfers between devices  57.8 us (32%)
  local copies, waits for them, and re-layouts  18.1 us (10%)
  Pallas kernels  16.1 us (9%)
  other arithmetic  5.8 us (3%)
    ppermute x29, starting transfers between devices, send(): return lax.ppermute(a, 'tensor', moves)  65.1 us
    ppermute x29, waiting for transfers between devices, send(): return lax.ppermute(a, 'tensor', moves)  50.7 us
    ppermute x5, starting transfers between devices, send_bulk(): return lax.ppermute(a, 'bulk', [(i, move(i)) for i in range(16)])  17.7 us
    pallas_call x1, Pallas kernels, last(): pl.pallas_call(functools.partial(last_body, steps), grid_spec=pltpu.Prefe...  12.7 us
    ppermute x5, waiting for transfers between devices, send_bulk(): return lax.ppermute(a, 'bulk', [(i, move(i)) for i in range(16)])  7.04 us
    unnamed x68, local copies, waits for them, and re-layouts  6.69 us
    dynamic_update_slice x8, local copies, waits for them, and re-layouts, join(): lax.dynamic_update_slice_in_dim(out, parts[d], (x + d) % NX * size, axis=2)  3.68 us
  transfers between devices with their start and end apart: 34, of which 14 were waited for; matrix products, arithmetic and copies ran while one was open for 8% of the time, Pallas kernels for 2%

profile of v3, /device:TPU:1, one launch (start us, length us, event | category | flops | bytes accessed | tf_op | source)
XLA Modules:
  0.0 182.2 jit_solution(9508227101017794968)
XLA Ops:
  2.5 2.1 %collective-permute-start = (bf16[4,16,2560]{2,1,0:T(8,128)(2,1)S(1)}, bf16[4,16,2560]{2,1,0:T(8,128)(2,1)S(1)}, u32[]{:S(2)}, u32[]{:S(2)}) collective-permute-start(bf16[4,16,2560]{2,1,0:T(8,128)(2,1)S(1)} %get-tuple-element.149), channel_id=1, source_target_pairs={{0,1},{1,2},{2,3},{3,0},{4,5},{5,6},{6,7},{7,4},{8,9},{9,10},{10,1... | collective-permute-start | bytes 983048 | tf_op jit(solution)/shard_map/ppermute | solution.py:32
  4.6 2.5 %collective-permute-start.1 = (bf16[4,16,2560]{2,1,0:T(8,128)(2,1)S(1)}, bf16[4,16,2560]{2,1,0:T(8,128)(2,1)S(1)}, u32[]{:S(2)}, u32[]{:S(2)}) collective-permute-start(bf16[4,16,2560]{2,1,0:T(8,128)(2,1)S(1)} %get-tuple-element.150), channel_id=1, source_target_pairs={{0,2},{1,3},{2,0},{3,1},{4,6},{5,7},{6,4},{7,5},{8,10},{9,11},{10,... | collective-permute-start | bytes 983048 | tf_op jit(solution)/shard_map/ppermute | solution.py:32
  11.2 10.0 %collective-permute-done.1 = bf16[4,16,2560]{2,1,0:T(8,128)(2,1)S(1)} collective-permute-done((bf16[4,16,2560]{2,1,0:T(8,128)(2,1)S(1)}, bf16[4,16,2560]{2,1,0:T(8,128)(2,1)S(1)}, u32[]{:S(2)}, u32[]{:S(2)}) %collective-permute-start.1) | collective-permute-done | bytes 327712 | tf_op jit(solution)/shard_map/ppermute | solution.py:32
  28.3 13.8 %collective-permute-done.3.refs_1_ = bf16[4,64,1792]{2,1,0:T(8,128)(2,1)S(1)} collective-permute-done((bf16[4,64,1792]{2,1,0:T(8,128)(2,1)S(1)}, bf16[4,64,1792]{2,1,0:T(8,128)(2,1)S(1)}, u32[]{:S(2)}, u32[]{:S(2)}) %collective-permute-start.3) | collective-permute-done | bytes 917536 | tf_op jit(solution)/shard_map/ppermute | solution.py:32
  45.0 8.5 %collective-permute-start.7 = (bf16[4,64,768]{2,1,0:T(8,128)(2,1)S(1)}, bf16[4,64,768]{2,1,0:T(8,128)(2,1)S(1)}, u32[]{:S(2)}, u32[]{:S(2)}) collective-permute-start(bf16[4,64,768]{2,1,0:T(8,128)(2,1)S(1)} %pad_maximum_fusion.10.refs_20_), channel_id=1, source_target_pairs={{0,4},{1,5},{2,6},{3,7},{12,8},{13,9},{14,10},{15,11},{16,20},{17,... | collective-permute-start | bytes 1179656 | tf_op jit(solution)/shard_map/ppermute | solution.py:32
  53.5 5.4 %collective-permute-done.9.refs_6_.refs_10_ = bf16[2,64,2816]{2,1,0:T(8,128)(2,1)S(1)} collective-permute-done((bf16[2,64,2816]{2,1,0:T(8,128)(2,1)S(1)}, bf16[2,64,2816]{2,1,0:T(8,128)(2,1)S(1)}, u32[]{:S(2)}, u32[]{:S(2)}) %collective-permute-start.9) | collective-permute-done | bytes 720928 | tf_op jit(solution)/shard_map/ppermute | solution.py:32
  60.1 7.0 %collective-permute-start.11 = (bf16[8,64,1024]{2,1,0:T(8,128)(2,1)}, bf16[8,64,1024]{2,1,0:T(8,128)(2,1)}, u32[]{:S(2)}, u32[]{:S(2)}) collective-permute-start(bf16[8,64,1024]{2,1,0:T(8,128)(2,1)} %pad_maximum_fusion), channel_id=1, source_target_pairs={{0,4},{1,5},{2,6},{3,7},{12,8},{13,9},{14,10},{15,11},{16,20},{17,... | collective-permute-start | bytes 3145736 | tf_op jit(solution)/shard_map/ppermute | solution.py:32
  78.3 3.4 %shard_map.93 = (bf16[2,64,1792]{2,1,0:T(8,128)(2,1)}, bf16[2,64,1792]{2,1,0:T(8,128)(2,1)}, bf16[2,64,1792]{2,1,0:T(8,128)(2,1)}, bf16[2,64,1792]{2,1,0:T(8,128...) custom-call(s32[17]{0:T(128)S(1)} %pad_add_fusion.info, ...), custom_call_target="tpu_custom_call" | custom-call | flops 2348810240 | bytes 18350080 | tf_op jit(solution)/shard_map/pallas_call | solution.py:141
  81.7 5.2 %collective-permute-done.11.refs_23_.refs_24_ = bf16[8,64,1024]{2,1,0:T(8,128)(2,1)} collective-permute-done((bf16[8,64,1024]{2,1,0:T(8,128)(2,1)}, bf16[8,64,1024]{2,1,0:T(8,128)(2,1)}, u32[]{:S(2)}, u32[]{:S(2)}) %collective-permute-start.11) | collective-permute-done | bytes 1048608 | tf_op jit(solution)/shard_map/ppermute | solution.py:32
  86.9 2.5 %collective-permute-done.13.refs_3_ = bf16[4,64,1792]{2,1,0:T(8,128)(2,1)} collective-permute-done((bf16[4,64,1792]{2,1,0:T(8,128)(2,1)}, bf16[4,64,1792]{2,1,0:T(8,128)(2,1)}, u32[]{:S(2)}, u32[]{:S(2)}) %collective-permute-start.13) | collective-permute-done | bytes 917536 | tf_op jit(solution)/shard_map/ppermute | solution.py:32
  89.5 12.7 %shard_map.94 = (bf16[2,64,1792]{2,1,0:T(8,128)(2,1)}, bf16[2,64,1792]{2,1,0:T(8,128)(2,1)}, bf16[2,64,1792]{2,1,0:T(8,128)(2,1)}, bf16[2,64,1792]{2,1,0:T(8,128...) custom-call(s32[17]{0:T(128)S(1)} %pad_add_fusion.info, ...), custom_call_target="tpu_custom_call", output_to_operand_aliasing={{0}: (13, {}), {1}: (14, {}), {2}: (15, {}), {3}: (16, {}),... | custom-call | flops 2348810240 | bytes 18350080 | tf_op jit(solution)/shard_map/pallas_call | solution.py:249
  103.6 4.1 %collective-permute-start.14 = (bf16[2,64,1792]{2,1,0:T(8,128)(2,1)}, bf16[2,64,1792]{2,1,0:T(8,128)(2,1)S(1)}, u32[]{:S(2)}, u32[]{:S(2)}) collective-permute-start(bf16[2,64,1792]{2,1,0:T(8,128)(2,1)} %get-tuple-element.105), channel_id=1, source_target_pairs={{0,4},{1,5},{2,6},{3,7},{12,8},{13,9},{14,10},{15,11},{16,20},{17,... | collective-permute-start | bytes 1376264 | tf_op jit(solution)/shard_map/ppermute | solution.py:32
  107.7 6.3 %collective-permute-start.17 = (bf16[2,64,1792]{2,1,0:T(8,128)(2,1)}, bf16[2,64,1792]{2,1,0:T(8,128)(2,1)S(1)}, u32[]{:S(2)}, u32[]{:S(2)}) collective-permute-start(bf16[2,64,1792]{2,1,0:T(8,128)(2,1)} %get-tuple-element.111), channel_id=1, source_target_pairs={{0,3},{1,0},{2,1},{3,2},{4,7},{5,4},{6,5},{7,6},{8,11},{9,8},{10,9... | collective-permute-start | bytes 1376264 | tf_op jit(solution)/shard_map/ppermute | solution.py:32
  116.2 4.4 %collective-permute-start.15 = (bf16[2,64,1792]{2,1,0:T(8,128)(2,1)S(1)}, bf16[2,64,1792]{2,1,0:T(8,128)(2,1)S(1)}, u32[]{:S(2)}, u32[]{:S(2)}) collective-permute-start(bf16[2,64,1792]{2,1,0:T(8,128)(2,1)S(1)} %copy-done.17), channel_id=1, source_target_pairs={{0,4},{1,5},{2,6},{3,7},{12,8},{13,9},{14,10},{15,11},{16,20},{17,... | collective-permute-start | bytes 1376264 | tf_op jit(solution)/shard_map/ppermute | solution.py:32
  120.6 3.9 %collective-permute-done.22 = bf16[8,64,1024]{2,1,0:T(8,128)(2,1)S(1)} collective-permute-done((bf16[8,64,1024]{2,1,0:T(8,128)(2,1)}, bf16[8,64,1024]{2,1,0:T(8,128)(2,1)S(1)}, u32[]{:S(2)}, u32[]{:S(2)}) %collective-permute-start.22) | collective-permute-done | bytes 1048608 | tf_op jit(solution)/shard_map/ppermute | solution.py:32
  125.5 2.6 %collective-permute-start.25 = (bf16[2,64,1024]{2,1,0:T(8,128)(2,1)S(1)}, bf16[2,64,1024]{2,1,0:T(8,128)(2,1)S(1)}, u32[]{:S(2)}, u32[]{:S(2)}) collective-permute-start(bf16[2,64,1024]{2,1,0:T(8,128)(2,1)S(1)} %maximum_select_fusion.3), channel_id=1, source_target_pairs={{0,1},{1,2},{2,3},{3,0},{4,5},{5,6},{6,7},{7,4},{8,9},{9,10},{10,1... | collective-permute-start | bytes 786440 | tf_op jit(solution)/shard_map/ppermute | solution.py:32
  128.5 6.0 %collective-permute-start.24 = (bf16[2,64,1024]{2,1,0:T(8,128)(2,1)S(1)}, bf16[2,64,1024]{2,1,0:T(8,128)(2,1)S(1)}, u32[]{:S(2)}, u32[]{:S(2)}) collective-permute-start(bf16[2,64,1024]{2,1,0:T(8,128)(2,1)S(1)} %maximum_select_fusion.2), channel_id=1, source_target_pairs={{0,2},{1,3},{2,0},{3,1},{4,6},{5,7},{6,4},{7,5},{8,10},{9,11},{10,... | collective-permute-start | bytes 786440 | tf_op jit(solution)/shard_map/ppermute | solution.py:32
  136.7 4.7 %collective-permute-done.24 = bf16[2,64,1024]{2,1,0:T(8,128)(2,1)S(1)} collective-permute-done((bf16[2,64,1024]{2,1,0:T(8,128)(2,1)S(1)}, bf16[2,64,1024]{2,1,0:T(8,128)(2,1)S(1)}, u32[]{:S(2)}, u32[]{:S(2)}) %collective-permute-start.24) | collective-permute-done | bytes 262176 | tf_op jit(solution)/shard_map/ppermute | solution.py:32
  141.6 5.6 %collective-permute-start.26 = (f32[64,256]{1,0:T(8,128)S(1)}, f32[64,256]{1,0:T(8,128)S(1)}, u32[]{:S(2)}, u32[]{:S(2)}) collective-permute-start(f32[64,256]{1,0:T(8,128)S(1)} %slice_bitcast_fusion.8), channel_id=1, source_target_pairs={{0,16},{16,0},{32,48},{48,32},{64,80},{80,64},{96,112},{112,96},{1... | collective-permute-start | bytes 196616 | tf_op jit(solution)/shard_map/ppermute | solution.py:36
  148.5 3.2 %collective-permute-start.27 = (f32[64,256]{1,0:T(8,128)S(1)}, f32[64,256]{1,0:T(8,128)S(1)}, u32[]{:S(2)}, u32[]{:S(2)}) collective-permute-start(f32[64,256]{1,0:T(8,128)S(1)} %fusion.16), channel_id=1, source_target_pairs={{0,64},{16,80},{32,96},{48,112},{64,0},{80,16},{96,32},{112,48},{1... | collective-permute-start | bytes 196616 | tf_op jit(solution)/shard_map/ppermute | solution.py:36
  157.2 4.3 %collective-permute-start.29 = (f32[64,256]{1,0:T(8,128)S(1)}, f32[64,256]{1,0:T(8,128)S(1)}, u32[]{:S(2)}, u32[]{:S(2)}) collective-permute-start(f32[64,256]{1,0:T(8,128)S(1)} %add.200), channel_id=1, source_target_pairs={{0,128},{16,144},{32,160},{48,176},{64,192},{80,208},{96,224},{112... | collective-permute-start | bytes 196616 | tf_op jit(solution)/shard_map/ppermute | solution.py:36
  161.5 2.9 %collective-permute-done.29 = f32[64,256]{1,0:T(8,128)S(1)} collective-permute-done((f32[64,256]{1,0:T(8,128)S(1)}, f32[64,256]{1,0:T(8,128)S(1)}, u32[]{:S(2)}, u32[]{:S(2)}) %collective-permute-start.29) | collective-permute-done | bytes 65568 | tf_op jit(solution)/shard_map/ppermute | solution.py:36
  164.5 3.2 %collective-permute-start.33 = (f32[64,256]{1,0:T(8,128)S(1)}, f32[64,256]{1,0:T(8,128)S(1)}, u32[]{:S(2)}, u32[]{:S(2)}) collective-permute-start(f32[64,256]{1,0:T(8,128)S(1)} %broadcast_multiply_fusion), channel_id=1, source_target_pairs={{0,16},{16,0},{32,48},{48,32},{64,80},{80,64},{96,112},{112,96},{1... | collective-permute-start | bytes 196616 | tf_op jit(solution)/shard_map/ppermute | solution.py:36
  170.0 2.3 %collective-permute-start.31 = (bf16[2,16,2560]{2,1,0:T(8,128)(2,1)S(1)}, bf16[2,16,2560]{2,1,0:T(8,128)(2,1)S(1)}, u32[]{:S(2)}, u32[]{:S(2)}) collective-permute-start(bf16[2,16,2560]{2,1,0:T(8,128)(2,1)S(1)} %get-tuple-element.161), channel_id=1, source_target_pairs={{0,2},{1,3},{2,0},{3,1},{4,6},{5,7},{6,4},{7,5},{8,10},{9,11},{10,... | collective-permute-start | bytes 491528 | tf_op jit(solution)/shard_map/ppermute | solution.py:32
  (188 shorter events, 54.0 us)
Async XLA Ops:
  4.6 16.6 %collective-permute-start.1 = (bf16[4,16,2560]{2,1,0:T(8,128)(2,1)S(1)}, bf16[4,16,2560]{2,1,0:T(8,128)(2,1)S(1)}, u32[]{:S(2)}, u32[]{:S(2)}) collective-permute-start(bf16[4,16,2560]{2,1,0:T(8,128)(2,1)S(1)} %get-tuple-element.150), channel_id=1, source_target_pairs={{0,2},{1,3},{2,0},{3,1},{4,6},{5,7},{6,4},{7,5},{8,10},{9,11},{10,... | collective-permute-start | bytes 983048 | tf_op jit(solution)/shard_map/ppermute | solution.py:32
  7.1 14.2 %collective-permute-start.2 = (bf16[4,16,2560]{2,1,0:T(8,128)(2,1)S(1)}, bf16[4,16,2560]{2,1,0:T(8,128)(2,1)S(1)}, u32[]{:S(2)}, u32[]{:S(2)}) collective-permute-start(bf16[4,16,2560]{2,1,0:T(8,128)(2,1)S(1)} %get-tuple-element.151), channel_id=1, source_target_pairs={{0,3},{1,0},{2,1},{3,2},{4,7},{5,4},{6,5},{7,6},{8,11},{9,8},{10,9... | collective-permute-start | bytes 983048 | tf_op jit(solution)/shard_map/ppermute | solution.py:32
  21.4 20.7 %collective-permute-start.3 = (bf16[4,64,1792]{2,1,0:T(8,128)(2,1)S(1)}, bf16[4,64,1792]{2,1,0:T(8,128)(2,1)S(1)}, u32[]{:S(2)}, u32[]{:S(2)}) collective-permute-start(bf16[4,64,1792]{2,1,0:T(8,128)(2,1)S(1)} %pad_maximum_fusion.1.refs_0_), channel_id=1, source_target_pairs={{0,4},{1,5},{2,6},{3,7},{4,0},{5,1},{6,2},{7,3},{8,12},{9,13},{10,... | collective-permute-start | bytes 2752520 | tf_op jit(solution)/shard_map/ppermute | solution.py:32
  23.1 19.0 %collective-permute-start.4 = (bf16[4,64,1792]{2,1,0:T(8,128)(2,1)S(1)}, bf16[4,64,1792]{2,1,0:T(8,128)(2,1)S(1)}, u32[]{:S(2)}, u32[]{:S(2)}) collective-permute-start(bf16[4,64,1792]{2,1,0:T(8,128)(2,1)S(1)} %pad_maximum_fusion.1.refs_0_), channel_id=1, source_target_pairs={{4,8},{5,9},{6,10},{7,11},{8,4},{9,5},{10,6},{11,7},{20,24},{21,25... | collective-permute-start | bytes 2752520 | tf_op jit(solution)/shard_map/ppermute | solution.py:32
  23.8 21.2 %collective-permute-start.8 = (bf16[2,64,2816]{2,1,0:T(8,128)(2,1)S(1)}, bf16[2,64,2816]{2,1,0:T(8,128)(2,1)S(1)}, u32[]{:S(2)}, u32[]{:S(2)}) collective-permute-start(bf16[2,64,2816]{2,1,0:T(8,128)(2,1)S(1)} %get-tuple-element.78), channel_id=1, source_target_pairs={{0,1},{1,2},{2,3},{3,0},{4,5},{5,6},{6,7},{7,4},{8,9},{9,10},{10,1... | collective-permute-start | bytes 2162696 | tf_op jit(solution)/shard_map/ppermute | solution.py:32
  25.2 33.7 %collective-permute-start.10 = (bf16[2,64,2816]{2,1,0:T(8,128)(2,1)S(1)}, bf16[2,64,2816]{2,1,0:T(8,128)(2,1)S(1)}, u32[]{:S(2)}, u32[]{:S(2)}) collective-permute-start(bf16[2,64,2816]{2,1,0:T(8,128)(2,1)S(1)} %get-tuple-element.80), channel_id=1, source_target_pairs={{0,3},{1,0},{2,1},{3,2},{4,7},{5,4},{6,5},{7,6},{8,11},{9,8},{10,9... | collective-permute-start | bytes 2162696 | tf_op jit(solution)/shard_map/ppermute | solution.py:32
  27.0 31.9 %collective-permute-start.9 = (bf16[2,64,2816]{2,1,0:T(8,128)(2,1)S(1)}, bf16[2,64,2816]{2,1,0:T(8,128)(2,1)S(1)}, u32[]{:S(2)}, u32[]{:S(2)}) collective-permute-start(bf16[2,64,2816]{2,1,0:T(8,128)(2,1)S(1)} %get-tuple-element.79), channel_id=1, source_target_pairs={{0,2},{1,3},{2,0},{3,1},{4,6},{5,7},{6,4},{7,5},{8,10},{9,11},{10,... | collective-permute-start | bytes 2162696 | tf_op jit(solution)/shard_map/ppermute | solution.py:32
  42.1 25.0 %collective-permute-start.5 = (bf16[4,64,1792]{2,1,0:T(8,128)(2,1)S(1)}, bf16[4,64,1792]{2,1,0:T(8,128)(2,1)}, u32[]{:S(2)}, u32[]{:S(2)}) collective-permute-start(bf16[4,64,1792]{2,1,0:T(8,128)(2,1)S(1)} %collective-permute-done.3.refs_1_), channel_id=1, source_target_pairs={{4,8},{5,9},{6,10},{7,11},{8,4},{9,5},{10,6},{11,7},{20,24},{21,25... | collective-permute-start | bytes 2752520 | tf_op jit(solution)/shard_map/ppermute | solution.py:32
  43.7 25.4 %collective-permute-start.6 = (bf16[4,64,1792]{2,1,0:T(8,128)(2,1)S(1)}, bf16[4,64,1792]{2,1,0:T(8,128)(2,1)S(1)}, u32[]{:S(2)}, u32[]{:S(2)}) collective-permute-start(bf16[4,64,1792]{2,1,0:T(8,128)(2,1)S(1)} %collective-permute-done.4.refs_2_), channel_id=1, source_target_pairs={{4,0},{5,1},{6,2},{7,3},{8,12},{9,13},{10,14},{11,15},{20,16},{21,... | collective-permute-start | bytes 2752520 | tf_op jit(solution)/shard_map/ppermute | solution.py:32
  45.0 22.1 %collective-permute-start.7 = (bf16[4,64,768]{2,1,0:T(8,128)(2,1)S(1)}, bf16[4,64,768]{2,1,0:T(8,128)(2,1)S(1)}, u32[]{:S(2)}, u32[]{:S(2)}) collective-permute-start(bf16[4,64,768]{2,1,0:T(8,128)(2,1)S(1)} %pad_maximum_fusion.10.refs_20_), channel_id=1, source_target_pairs={{0,4},{1,5},{2,6},{3,7},{12,8},{13,9},{14,10},{15,11},{16,20},{17,... | collective-permute-start | bytes 1179656 | tf_op jit(solution)/shard_map/ppermute | solution.py:32
  60.1 26.8 %collective-permute-start.11 = (bf16[8,64,1024]{2,1,0:T(8,128)(2,1)}, bf16[8,64,1024]{2,1,0:T(8,128)(2,1)}, u32[]{:S(2)}, u32[]{:S(2)}) collective-permute-start(bf16[8,64,1024]{2,1,0:T(8,128)(2,1)} %pad_maximum_fusion), channel_id=1, source_target_pairs={{0,4},{1,5},{2,6},{3,7},{12,8},{13,9},{14,10},{15,11},{16,20},{17,... | collective-permute-start | bytes 3145736 | tf_op jit(solution)/shard_map/ppermute | solution.py:32
  69.1 20.4 %collective-permute-start.13 = (bf16[4,64,1792]{2,1,0:T(8,128)(2,1)}, bf16[4,64,1792]{2,1,0:T(8,128)(2,1)}, u32[]{:S(2)}, u32[]{:S(2)}) collective-permute-start(bf16[4,64,1792]{2,1,0:T(8,128)(2,1)} %collective-permute-done.5.refs_3_), channel_id=1, source_target_pairs={{4,0},{5,1},{6,2},{7,3},{8,12},{9,13},{10,14},{11,15},{20,16},{21,... | collective-permute-start | bytes 2752520 | tf_op jit(solution)/shard_map/ppermute | solution.py:32
  72.2 14.8 %collective-permute-start.12 = (bf16[8,64,768]{2,1,0:T(8,128)(2,1)}, bf16[8,64,768]{2,1,0:T(8,128)(2,1)}, u32[]{:S(2)}, u32[]{:S(2)}) collective-permute-start(bf16[8,64,768]{2,1,0:T(8,128)(2,1)} %pad_maximum_fusion.2), channel_id=1, source_target_pairs={{4,8},{5,9},{6,10},{7,11},{8,4},{9,5},{10,6},{11,7},{20,24},{21,25... | collective-permute-start | bytes 2359304 | tf_op jit(solution)/shard_map/ppermute | solution.py:32
  102.2 22.3 %collective-permute-start.22 = (bf16[8,64,1024]{2,1,0:T(8,128)(2,1)}, bf16[8,64,1024]{2,1,0:T(8,128)(2,1)S(1)}, u32[]{:S(2)}, u32[]{:S(2)}) collective-permute-start(bf16[8,64,1024]{2,1,0:T(8,128)(2,1)} %get-tuple-element.125), channel_id=1, source_target_pairs={{4,0},{5,1},{6,2},{7,3},{8,12},{9,13},{10,14},{11,15},{20,16},{21,... | collective-permute-start | bytes 3145736 | tf_op jit(solution)/shard_map/ppermute | solution.py:32
  103.6 11.5 %collective-permute-start.14 = (bf16[2,64,1792]{2,1,0:T(8,128)(2,1)}, bf16[2,64,1792]{2,1,0:T(8,128)(2,1)S(1)}, u32[]{:S(2)}, u32[]{:S(2)}) collective-permute-start(bf16[2,64,1792]{2,1,0:T(8,128)(2,1)} %get-tuple-element.105), channel_id=1, source_target_pairs={{0,4},{1,5},{2,6},{3,7},{12,8},{13,9},{14,10},{15,11},{16,20},{17,... | collective-permute-start | bytes 1376264 | tf_op jit(solution)/shard_map/ppermute | solution.py:32
  107.7 20.8 %collective-permute-start.17 = (bf16[2,64,1792]{2,1,0:T(8,128)(2,1)}, bf16[2,64,1792]{2,1,0:T(8,128)(2,1)S(1)}, u32[]{:S(2)}, u32[]{:S(2)}) collective-permute-start(bf16[2,64,1792]{2,1,0:T(8,128)(2,1)} %get-tuple-element.111), channel_id=1, source_target_pairs={{0,3},{1,0},{2,1},{3,2},{4,7},{5,4},{6,5},{7,6},{8,11},{9,8},{10,9... | collective-permute-start | bytes 1376264 | tf_op jit(solution)/shard_map/ppermute | solution.py:32
  114.0 20.5 %collective-permute-start.18 = (bf16[2,64,1792]{2,1,0:T(8,128)(2,1)}, bf16[2,64,1792]{2,1,0:T(8,128)(2,1)S(1)}, u32[]{:S(2)}, u32[]{:S(2)}) collective-permute-start(bf16[2,64,1792]{2,1,0:T(8,128)(2,1)} %get-tuple-element.113), channel_id=1, source_target_pairs={{0,1},{1,2},{2,3},{3,0},{4,5},{5,6},{6,7},{7,4},{8,9},{9,10},{10,1... | collective-permute-start | bytes 1376264 | tf_op jit(solution)/shard_map/ppermute | solution.py:32
  115.3 19.2 %collective-permute-start.16 = (bf16[2,64,2560]{2,1,0:T(8,128)(2,1)S(1)}, bf16[2,64,2560]{2,1,0:T(8,128)(2,1)S(1)}, u32[]{:S(2)}, u32[]{:S(2)}) collective-permute-start(bf16[2,64,2560]{2,1,0:T(8,128)(2,1)S(1)} %pad_maximum_fusion.4), channel_id=1, source_target_pairs={{4,8},{5,9},{6,10},{7,11},{8,4},{9,5},{10,6},{11,7},{20,24},{21,25... | collective-permute-start | bytes 1966088 | tf_op jit(solution)/shard_map/ppermute | solution.py:32
  116.2 18.3 %collective-permute-start.15 = (bf16[2,64,1792]{2,1,0:T(8,128)(2,1)S(1)}, bf16[2,64,1792]{2,1,0:T(8,128)(2,1)S(1)}, u32[]{:S(2)}, u32[]{:S(2)}) collective-permute-start(bf16[2,64,1792]{2,1,0:T(8,128)(2,1)S(1)} %copy-done.17), channel_id=1, source_target_pairs={{0,4},{1,5},{2,6},{3,7},{12,8},{13,9},{14,10},{15,11},{16,20},{17,... | collective-permute-start | bytes 1376264 | tf_op jit(solution)/shard_map/ppermute | solution.py:32
  128.5 12.9 %collective-permute-start.24 = (bf16[2,64,1024]{2,1,0:T(8,128)(2,1)S(1)}, bf16[2,64,1024]{2,1,0:T(8,128)(2,1)S(1)}, u32[]{:S(2)}, u32[]{:S(2)}) collective-permute-start(bf16[2,64,1024]{2,1,0:T(8,128)(2,1)S(1)} %maximum_select_fusion.2), channel_id=1, source_target_pairs={{0,2},{1,3},{2,0},{3,1},{4,6},{5,7},{6,4},{7,5},{8,10},{9,11},{10,... | collective-permute-start | bytes 786440 | tf_op jit(solution)/shard_map/ppermute | solution.py:32
  134.7 29.8 %collective-permute-start.20 = (bf16[2,64,2560]{2,1,0:T(8,128)(2,1)S(1)}, bf16[2,64,2560]{2,1,0:T(8,128)(2,1)S(1)}, u32[]{:S(2)}, u32[]{:S(2)}) collective-permute-start(bf16[2,64,2560]{2,1,0:T(8,128)(2,1)S(1)} %add_convert_fusion.1), channel_id=1, source_target_pairs={{0,4},{1,5},{2,6},{3,7},{4,0},{5,1},{6,2},{7,3},{8,12},{9,13},{10,... | collective-permute-start | bytes 1966088 | tf_op jit(solution)/shard_map/ppermute | solution.py:32
  147.2 17.2 %collective-permute-start.19 = (bf16[2,64,2560]{2,1,0:T(8,128)(2,1)S(1)}, bf16[2,64,2560]{2,1,0:T(8,128)(2,1)S(1)}, u32[]{:S(2)}, u32[]{:S(2)}) collective-permute-start(bf16[2,64,2560]{2,1,0:T(8,128)(2,1)S(1)} %pad_maximum_fusion.5), channel_id=1, source_target_pairs={{4,8},{5,9},{6,10},{7,11},{8,4},{9,5},{10,6},{11,7},{20,24},{21,25... | collective-permute-start | bytes 1966088 | tf_op jit(solution)/shard_map/ppermute | solution.py:32
  148.0 16.5 %collective-permute-start.21 = (bf16[2,64,1792]{2,1,0:T(8,128)(2,1)S(1)}, bf16[2,64,1792]{2,1,0:T(8,128)(2,1)S(1)}, u32[]{:S(2)}, u32[]{:S(2)}) collective-permute-start(bf16[2,64,1792]{2,1,0:T(8,128)(2,1)S(1)} %copy-done.26), channel_id=1, source_target_pairs={{0,2},{1,3},{2,0},{3,1},{4,6},{5,7},{6,4},{7,5},{8,10},{9,11},{10,... | collective-permute-start | bytes 1376264 | tf_op jit(solution)/shard_map/ppermute | solution.py:32
  164.5 13.9 %collective-permute-start.33 = (f32[64,256]{1,0:T(8,128)S(1)}, f32[64,256]{1,0:T(8,128)S(1)}, u32[]{:S(2)}, u32[]{:S(2)}) collective-permute-start(f32[64,256]{1,0:T(8,128)S(1)} %broadcast_multiply_fusion), channel_id=1, source_target_pairs={{0,16},{16,0},{32,48},{48,32},{64,80},{80,64},{96,112},{112,96},{1... | collective-permute-start | bytes 196616 | tf_op jit(solution)/shard_map/ppermute | solution.py:36
  (48 other events, 457.6 us)

commit v4 on v3

--- a/solution.py
+++ b/solution.py
@@ -358,13 +358,12 @@
     mine = mine + send_bulk(other, lambda i: i ^ 1)
     mine = mine + send_bulk(mine, lambda i: i ^ 4)
     mine = mine + send_bulk(mine, lambda i: i ^ 2)
-    mine = mine + send_bulk(mine, lambda i: i ^ 8)
     c, near, gm_a, gm_b, mine = together(c, near, gm_a, gm_b, mine)
     own = jnp.concatenate([own, jnp.where(middle, gs_own, zero)], axis=2).astype(F32)
     own = (own + c.astype(F32) + near.astype(F32)).astype(BF)
     own = [own[:, 16 * i : 16 * i + 16] for i in range(NX)]
     own = [own[0]] + [send(own[i], x_shift(-i)) for i in range(1, NX)]
-    mine = scale * mine
+    mine = scale * (mine + send_bulk(mine, lambda i: i ^ 8))
     other = send_bulk(mine, lambda i: i ^ 1)
     grad_in = jnp.where(core == 0, mine, other)
     grad_out = jnp.where(core == 0, other, mine)

time: 183 us -> 180 us (0.984)
  starting transfers between devices: 82.8 us -> 80 us
    ppermute x29, waiting for transfers between devices: 50.7 us -> 52.9 us  [send(): return lax.ppermute(a, 'tensor', moves)]
    ppermute x5, waiting for transfers between devices: 7.04 us -> 4.95 us  [send_bulk(): return lax.ppermute(a, 'bulk', [(i, move(i)) for i in range(16)])]
  transfers between devices with their start and end apart: 34 -> 34, of which waited for: 14 -> 16; matrix products, arithmetic and copies ran while one was open for 8% -> 8% of each run, Pallas kernels for 2% -> 2%
where the time goes in v4:
time: 180 us; the launch traced here: 179 us
  starting transfers between devices  80 us (44%)
  waiting for transfers between devices  57.8 us (32%)
  local copies, waits for them, and re-layouts  18.1 us (10%)
  Pallas kernels  16.1 us (9%)
  other arithmetic  5.51 us (3%)
    ppermute x29, starting transfers between devices, send(): return lax.ppermute(a, 'tensor', moves)  63.9 us
    ppermute x29, waiting for transfers between devices, send(): return lax.ppermute(a, 'tensor', moves)  52.9 us
    ppermute x5, starting transfers between devices, send_bulk(): return lax.ppermute(a, 'bulk', [(i, move(i)) for i in range(16)])  16.2 us
    pallas_call x1, Pallas kernels, last(): pl.pallas_call(functools.partial(last_body, steps), grid_spec=pltpu.Prefe...  12.7 us
    unnamed x68, local copies, waits for them, and re-layouts  7.34 us
    ppermute x5, waiting for transfers between devices, send_bulk(): return lax.ppermute(a, 'bulk', [(i, move(i)) for i in range(16)])  4.95 us
    dynamic_update_slice x8, local copies, waits for them, and re-layouts, join(): lax.dynamic_update_slice_in_dim(out, parts[d], (x + d) % NX * size, axis=2)  3.68 us
  transfers between devices with their start and end apart: 34, of which 16 were waited for; matrix products, arithmetic and copies ran while one was open for 8% of the time, Pallas kernels for 2%

profile of v4, /device:TPU:1, one launch (start us, length us, event | category | flops | bytes accessed | tf_op | source)
XLA Modules:
  0.0 179.1 jit_solution(12695062160292774447)
XLA Ops:
  2.5 2.1 %collective-permute-start = (bf16[4,16,2560]{2,1,0:T(8,128)(2,1)S(1)}, bf16[4,16,2560]{2,1,0:T(8,128)(2,1)S(1)}, u32[]{:S(2)}, u32[]{:S(2)}) collective-permute-start(bf16[4,16,2560]{2,1,0:T(8,128)(2,1)S(1)} %get-tuple-element.149), channel_id=1, source_target_pairs={{0,1},{1,2},{2,3},{3,0},{4,5},{5,6},{6,7},{7,4},{8,9},{9,10},{10,1... | collective-permute-start | bytes 983048 | tf_op jit(solution)/shard_map/ppermute | solution.py:32
  4.6 2.5 %collective-permute-start.1 = (bf16[4,16,2560]{2,1,0:T(8,128)(2,1)S(1)}, bf16[4,16,2560]{2,1,0:T(8,128)(2,1)S(1)}, u32[]{:S(2)}, u32[]{:S(2)}) collective-permute-start(bf16[4,16,2560]{2,1,0:T(8,128)(2,1)S(1)} %get-tuple-element.150), channel_id=1, source_target_pairs={{0,2},{1,3},{2,0},{3,1},{4,6},{5,7},{6,4},{7,5},{8,10},{9,11},{10,... | collective-permute-start | bytes 983048 | tf_op jit(solution)/shard_map/ppermute | solution.py:32
  11.2 10.0 %collective-permute-done.1 = bf16[4,16,2560]{2,1,0:T(8,128)(2,1)S(1)} collective-permute-done((bf16[4,16,2560]{2,1,0:T(8,128)(2,1)S(1)}, bf16[4,16,2560]{2,1,0:T(8,128)(2,1)S(1)}, u32[]{:S(2)}, u32[]{:S(2)}) %collective-permute-start.1) | collective-permute-done | bytes 327712 | tf_op jit(solution)/shard_map/ppermute | solution.py:32
  28.3 13.8 %collective-permute-done.3.refs_1_ = bf16[4,64,1792]{2,1,0:T(8,128)(2,1)S(1)} collective-permute-done((bf16[4,64,1792]{2,1,0:T(8,128)(2,1)S(1)}, bf16[4,64,1792]{2,1,0:T(8,128)(2,1)S(1)}, u32[]{:S(2)}, u32[]{:S(2)}) %collective-permute-start.3) | collective-permute-done | bytes 917536 | tf_op jit(solution)/shard_map/ppermute | solution.py:32
  45.0 8.5 %collective-permute-start.7 = (bf16[4,64,768]{2,1,0:T(8,128)(2,1)S(1)}, bf16[4,64,768]{2,1,0:T(8,128)(2,1)S(1)}, u32[]{:S(2)}, u32[]{:S(2)}) collective-permute-start(bf16[4,64,768]{2,1,0:T(8,128)(2,1)S(1)} %pad_maximum_fusion.10.refs_20_), channel_id=1, source_target_pairs={{0,4},{1,5},{2,6},{3,7},{12,8},{13,9},{14,10},{15,11},{16,20},{17,... | collective-permute-start | bytes 1179656 | tf_op jit(solution)/shard_map/ppermute | solution.py:32
  53.5 5.4 %collective-permute-done.9.refs_6_.refs_10_ = bf16[2,64,2816]{2,1,0:T(8,128)(2,1)S(1)} collective-permute-done((bf16[2,64,2816]{2,1,0:T(8,128)(2,1)S(1)}, bf16[2,64,2816]{2,1,0:T(8,128)(2,1)S(1)}, u32[]{:S(2)}, u32[]{:S(2)}) %collective-permute-start.9) | collective-permute-done | bytes 720928 | tf_op jit(solution)/shard_map/ppermute | solution.py:32
  60.1 7.0 %collective-permute-start.11 = (bf16[8,64,1024]{2,1,0:T(8,128)(2,1)}, bf16[8,64,1024]{2,1,0:T(8,128)(2,1)}, u32[]{:S(2)}, u32[]{:S(2)}) collective-permute-start(bf16[8,64,1024]{2,1,0:T(8,128)(2,1)} %pad_maximum_fusion), channel_id=1, source_target_pairs={{0,4},{1,5},{2,6},{3,7},{12,8},{13,9},{14,10},{15,11},{16,20},{17,... | collective-permute-start | bytes 3145736 | tf_op jit(solution)/shard_map/ppermute | solution.py:32
  78.3 3.4 %shard_map.93 = (bf16[2,64,1792]{2,1,0:T(8,128)(2,1)}, bf16[2,64,1792]{2,1,0:T(8,128)(2,1)}, bf16[2,64,1792]{2,1,0:T(8,128)(2,1)}, bf16[2,64,1792]{2,1,0:T(8,128...) custom-call(s32[17]{0:T(128)S(1)} %pad_add_fusion.info, ...), custom_call_target="tpu_custom_call" | custom-call | flops 2348810240 | bytes 18350080 | tf_op jit(solution)/shard_map/pallas_call | solution.py:141
  81.7 5.2 %collective-permute-done.11.refs_23_.refs_24_ = bf16[8,64,1024]{2,1,0:T(8,128)(2,1)} collective-permute-done((bf16[8,64,1024]{2,1,0:T(8,128)(2,1)}, bf16[8,64,1024]{2,1,0:T(8,128)(2,1)}, u32[]{:S(2)}, u32[]{:S(2)}) %collective-permute-start.11) | collective-permute-done | bytes 1048608 | tf_op jit(solution)/shard_map/ppermute | solution.py:32
  86.9 2.5 %collective-permute-done.13.refs_3_ = bf16[4,64,1792]{2,1,0:T(8,128)(2,1)} collective-permute-done((bf16[4,64,1792]{2,1,0:T(8,128)(2,1)}, bf16[4,64,1792]{2,1,0:T(8,128)(2,1)}, u32[]{:S(2)}, u32[]{:S(2)}) %collective-permute-start.13) | collective-permute-done | bytes 917536 | tf_op jit(solution)/shard_map/ppermute | solution.py:32
  89.5 12.7 %shard_map.94 = (bf16[2,64,1792]{2,1,0:T(8,128)(2,1)}, bf16[2,64,1792]{2,1,0:T(8,128)(2,1)}, bf16[2,64,1792]{2,1,0:T(8,128)(2,1)}, bf16[2,64,1792]{2,1,0:T(8,128...) custom-call(s32[17]{0:T(128)S(1)} %pad_add_fusion.info, ...), custom_call_target="tpu_custom_call", output_to_operand_aliasing={{0}: (13, {}), {1}: (14, {}), {2}: (15, {}), {3}: (16, {}),... | custom-call | flops 2348810240 | bytes 18350080 | tf_op jit(solution)/shard_map/pallas_call | solution.py:249
  103.6 4.1 %collective-permute-start.14 = (bf16[2,64,1792]{2,1,0:T(8,128)(2,1)}, bf16[2,64,1792]{2,1,0:T(8,128)(2,1)S(1)}, u32[]{:S(2)}, u32[]{:S(2)}) collective-permute-start(bf16[2,64,1792]{2,1,0:T(8,128)(2,1)} %get-tuple-element.105), channel_id=1, source_target_pairs={{0,4},{1,5},{2,6},{3,7},{12,8},{13,9},{14,10},{15,11},{16,20},{17,... | collective-permute-start | bytes 1376264 | tf_op jit(solution)/shard_map/ppermute | solution.py:32
  107.7 6.3 %collective-permute-start.17 = (bf16[2,64,1792]{2,1,0:T(8,128)(2,1)}, bf16[2,64,1792]{2,1,0:T(8,128)(2,1)S(1)}, u32[]{:S(2)}, u32[]{:S(2)}) collective-permute-start(bf16[2,64,1792]{2,1,0:T(8,128)(2,1)} %get-tuple-element.111), channel_id=1, source_target_pairs={{0,3},{1,0},{2,1},{3,2},{4,7},{5,4},{6,5},{7,6},{8,11},{9,8},{10,9... | collective-permute-start | bytes 1376264 | tf_op jit(solution)/shard_map/ppermute | solution.py:32
  116.2 4.4 %collective-permute-start.15 = (bf16[2,64,1792]{2,1,0:T(8,128)(2,1)S(1)}, bf16[2,64,1792]{2,1,0:T(8,128)(2,1)S(1)}, u32[]{:S(2)}, u32[]{:S(2)}) collective-permute-start(bf16[2,64,1792]{2,1,0:T(8,128)(2,1)S(1)} %copy-done.17), channel_id=1, source_target_pairs={{0,4},{1,5},{2,6},{3,7},{12,8},{13,9},{14,10},{15,11},{16,20},{17,... | collective-permute-start | bytes 1376264 | tf_op jit(solution)/shard_map/ppermute | solution.py:32
  120.6 3.9 %collective-permute-done.22 = bf16[8,64,1024]{2,1,0:T(8,128)(2,1)S(1)} collective-permute-done((bf16[8,64,1024]{2,1,0:T(8,128)(2,1)}, bf16[8,64,1024]{2,1,0:T(8,128)(2,1)S(1)}, u32[]{:S(2)}, u32[]{:S(2)}) %collective-permute-start.22) | collective-permute-done | bytes 1048608 | tf_op jit(solution)/shard_map/ppermute | solution.py:32
  125.5 2.6 %collective-permute-start.25 = (bf16[2,64,1024]{2,1,0:T(8,128)(2,1)S(1)}, bf16[2,64,1024]{2,1,0:T(8,128)(2,1)S(1)}, u32[]{:S(2)}, u32[]{:S(2)}) collective-permute-start(bf16[2,64,1024]{2,1,0:T(8,128)(2,1)S(1)} %maximum_select_fusion.3), channel_id=1, source_target_pairs={{0,1},{1,2},{2,3},{3,0},{4,5},{5,6},{6,7},{7,4},{8,9},{9,10},{10,1... | collective-permute-start | bytes 786440 | tf_op jit(solution)/shard_map/ppermute | solution.py:32
  128.5 6.0 %collective-permute-start.24 = (bf16[2,64,1024]{2,1,0:T(8,128)(2,1)S(1)}, bf16[2,64,1024]{2,1,0:T(8,128)(2,1)S(1)}, u32[]{:S(2)}, u32[]{:S(2)}) collective-permute-start(bf16[2,64,1024]{2,1,0:T(8,128)(2,1)S(1)} %maximum_select_fusion.2), channel_id=1, source_target_pairs={{0,2},{1,3},{2,0},{3,1},{4,6},{5,7},{6,4},{7,5},{8,10},{9,11},{10,... | collective-permute-start | bytes 786440 | tf_op jit(solution)/shard_map/ppermute | solution.py:32
  136.7 4.7 %collective-permute-done.24 = bf16[2,64,1024]{2,1,0:T(8,128)(2,1)S(1)} collective-permute-done((bf16[2,64,1024]{2,1,0:T(8,128)(2,1)S(1)}, bf16[2,64,1024]{2,1,0:T(8,128)(2,1)S(1)}, u32[]{:S(2)}, u32[]{:S(2)}) %collective-permute-start.24) | collective-permute-done | bytes 262176 | tf_op jit(solution)/shard_map/ppermute | solution.py:32
  141.6 5.6 %collective-permute-start.26 = (f32[64,256]{1,0:T(8,128)S(1)}, f32[64,256]{1,0:T(8,128)S(1)}, u32[]{:S(2)}, u32[]{:S(2)}) collective-permute-start(f32[64,256]{1,0:T(8,128)S(1)} %slice_bitcast_fusion.8), channel_id=1, source_target_pairs={{0,16},{16,0},{32,48},{48,32},{64,80},{80,64},{96,112},{112,96},{1... | collective-permute-start | bytes 196616 | tf_op jit(solution)/shard_map/ppermute | solution.py:36
  148.1 3.2 %collective-permute-start.27 = (f32[64,256]{1,0:T(8,128)S(1)}, f32[64,256]{1,0:T(8,128)S(1)}, u32[]{:S(2)}, u32[]{:S(2)}) collective-permute-start(f32[64,256]{1,0:T(8,128)S(1)} %fusion.16), channel_id=1, source_target_pairs={{0,64},{16,80},{32,96},{48,112},{64,0},{80,16},{96,32},{112,48},{1... | collective-permute-start | bytes 196616 | tf_op jit(solution)/shard_map/ppermute | solution.py:36
  154.8 2.1 %collective-permute-done.28 = f32[64,256]{1,0:T(8,128)S(1)} collective-permute-done((f32[64,256]{1,0:T(8,128)S(1)}, f32[64,256]{1,0:T(8,128)S(1)}, u32[]{:S(2)}, u32[]{:S(2)}) %collective-permute-start.28) | collective-permute-done | bytes 65568 | tf_op jit(solution)/shard_map/ppermute | solution.py:36
  156.9 3.9 %collective-permute-done.21 = bf16[2,64,1792]{2,1,0:T(8,128)(2,1)S(1)} collective-permute-done((bf16[2,64,1792]{2,1,0:T(8,128)(2,1)S(1)}, bf16[2,64,1792]{2,1,0:T(8,128)(2,1)S(1)}, u32[]{:S(2)}, u32[]{:S(2)}) %collective-permute-start.21) | collective-permute-done | bytes 458784 | tf_op jit(solution)/shard_map/ppermute | solution.py:32
  160.8 4.2 %collective-permute-start.32 = (f32[64,256]{1,0:T(8,128)S(1)}, f32[64,256]{1,0:T(8,128)S(1)}, u32[]{:S(2)}, u32[]{:S(2)}) collective-permute-start(f32[64,256]{1,0:T(8,128)S(1)} %add.200), channel_id=1, source_target_pairs={{0,128},{16,144},{32,160},{48,176},{64,192},{80,208},{96,224},{112... | collective-permute-start | bytes 196616 | tf_op jit(solution)/shard_map/ppermute | solution.py:36
  165.4 2.2 %collective-permute-start.29 = (bf16[2,16,2560]{2,1,0:T(8,128)(2,1)S(1)}, bf16[2,16,2560]{2,1,0:T(8,128)(2,1)S(1)}, u32[]{:S(2)}, u32[]{:S(2)}) collective-permute-start(bf16[2,16,2560]{2,1,0:T(8,128)(2,1)S(1)} %get-tuple-element.162), channel_id=1, source_target_pairs={{0,3},{1,0},{2,1},{3,2},{4,7},{5,4},{6,5},{7,6},{8,11},{9,8},{10,9... | collective-permute-start | bytes 491528 | tf_op jit(solution)/shard_map/ppermute | solution.py:32
  (187 shorter events, 51.2 us)
Async XLA Ops:
  4.6 16.6 %collective-permute-start.1 = (bf16[4,16,2560]{2,1,0:T(8,128)(2,1)S(1)}, bf16[4,16,2560]{2,1,0:T(8,128)(2,1)S(1)}, u32[]{:S(2)}, u32[]{:S(2)}) collective-permute-start(bf16[4,16,2560]{2,1,0:T(8,128)(2,1)S(1)} %get-tuple-element.150), channel_id=1, source_target_pairs={{0,2},{1,3},{2,0},{3,1},{4,6},{5,7},{6,4},{7,5},{8,10},{9,11},{10,... | collective-permute-start | bytes 983048 | tf_op jit(solution)/shard_map/ppermute | solution.py:32
  7.1 14.2 %collective-permute-start.2 = (bf16[4,16,2560]{2,1,0:T(8,128)(2,1)S(1)}, bf16[4,16,2560]{2,1,0:T(8,128)(2,1)S(1)}, u32[]{:S(2)}, u32[]{:S(2)}) collective-permute-start(bf16[4,16,2560]{2,1,0:T(8,128)(2,1)S(1)} %get-tuple-element.151), channel_id=1, source_target_pairs={{0,3},{1,0},{2,1},{3,2},{4,7},{5,4},{6,5},{7,6},{8,11},{9,8},{10,9... | collective-permute-start | bytes 983048 | tf_op jit(solution)/shard_map/ppermute | solution.py:32
  21.4 20.7 %collective-permute-start.3 = (bf16[4,64,1792]{2,1,0:T(8,128)(2,1)S(1)}, bf16[4,64,1792]{2,1,0:T(8,128)(2,1)S(1)}, u32[]{:S(2)}, u32[]{:S(2)}) collective-permute-start(bf16[4,64,1792]{2,1,0:T(8,128)(2,1)S(1)} %pad_maximum_fusion.1.refs_0_), channel_id=1, source_target_pairs={{0,4},{1,5},{2,6},{3,7},{4,0},{5,1},{6,2},{7,3},{8,12},{9,13},{10,... | collective-permute-start | bytes 2752520 | tf_op jit(solution)/shard_map/ppermute | solution.py:32
  23.1 19.0 %collective-permute-start.4 = (bf16[4,64,1792]{2,1,0:T(8,128)(2,1)S(1)}, bf16[4,64,1792]{2,1,0:T(8,128)(2,1)S(1)}, u32[]{:S(2)}, u32[]{:S(2)}) collective-permute-start(bf16[4,64,1792]{2,1,0:T(8,128)(2,1)S(1)} %pad_maximum_fusion.1.refs_0_), channel_id=1, source_target_pairs={{4,8},{5,9},{6,10},{7,11},{8,4},{9,5},{10,6},{11,7},{20,24},{21,25... | collective-permute-start | bytes 2752520 | tf_op jit(solution)/shard_map/ppermute | solution.py:32
  23.8 21.2 %collective-permute-start.8 = (bf16[2,64,2816]{2,1,0:T(8,128)(2,1)S(1)}, bf16[2,64,2816]{2,1,0:T(8,128)(2,1)S(1)}, u32[]{:S(2)}, u32[]{:S(2)}) collective-permute-start(bf16[2,64,2816]{2,1,0:T(8,128)(2,1)S(1)} %get-tuple-element.78), channel_id=1, source_target_pairs={{0,1},{1,2},{2,3},{3,0},{4,5},{5,6},{6,7},{7,4},{8,9},{9,10},{10,1... | collective-permute-start | bytes 2162696 | tf_op jit(solution)/shard_map/ppermute | solution.py:32
  25.2 33.7 %collective-permute-start.10 = (bf16[2,64,2816]{2,1,0:T(8,128)(2,1)S(1)}, bf16[2,64,2816]{2,1,0:T(8,128)(2,1)S(1)}, u32[]{:S(2)}, u32[]{:S(2)}) collective-permute-start(bf16[2,64,2816]{2,1,0:T(8,128)(2,1)S(1)} %get-tuple-element.80), channel_id=1, source_target_pairs={{0,3},{1,0},{2,1},{3,2},{4,7},{5,4},{6,5},{7,6},{8,11},{9,8},{10,9... | collective-permute-start | bytes 2162696 | tf_op jit(solution)/shard_map/ppermute | solution.py:32
  27.0 31.9 %collective-permute-start.9 = (bf16[2,64,2816]{2,1,0:T(8,128)(2,1)S(1)}, bf16[2,64,2816]{2,1,0:T(8,128)(2,1)S(1)}, u32[]{:S(2)}, u32[]{:S(2)}) collective-permute-start(bf16[2,64,2816]{2,1,0:T(8,128)(2,1)S(1)} %get-tuple-element.79), channel_id=1, source_target_pairs={{0,2},{1,3},{2,0},{3,1},{4,6},{5,7},{6,4},{7,5},{8,10},{9,11},{10,... | collective-permute-start | bytes 2162696 | tf_op jit(solution)/shard_map/ppermute | solution.py:32
  42.1 25.0 %collective-permute-start.5 = (bf16[4,64,1792]{2,1,0:T(8,128)(2,1)S(1)}, bf16[4,64,1792]{2,1,0:T(8,128)(2,1)}, u32[]{:S(2)}, u32[]{:S(2)}) collective-permute-start(bf16[4,64,1792]{2,1,0:T(8,128)(2,1)S(1)} %collective-permute-done.3.refs_1_), channel_id=1, source_target_pairs={{4,8},{5,9},{6,10},{7,11},{8,4},{9,5},{10,6},{11,7},{20,24},{21,25... | collective-permute-start | bytes 2752520 | tf_op jit(solution)/shard_map/ppermute | solution.py:32
  43.7 25.4 %collective-permute-start.6 = (bf16[4,64,1792]{2,1,0:T(8,128)(2,1)S(1)}, bf16[4,64,1792]{2,1,0:T(8,128)(2,1)S(1)}, u32[]{:S(2)}, u32[]{:S(2)}) collective-permute-start(bf16[4,64,1792]{2,1,0:T(8,128)(2,1)S(1)} %collective-permute-done.4.refs_2_), channel_id=1, source_target_pairs={{4,0},{5,1},{6,2},{7,3},{8,12},{9,13},{10,14},{11,15},{20,16},{21,... | collective-permute-start | bytes 2752520 | tf_op jit(solution)/shard_map/ppermute | solution.py:32
  45.0 22.1 %collective-permute-start.7 = (bf16[4,64,768]{2,1,0:T(8,128)(2,1)S(1)}, bf16[4,64,768]{2,1,0:T(8,128)(2,1)S(1)}, u32[]{:S(2)}, u32[]{:S(2)}) collective-permute-start(bf16[4,64,768]{2,1,0:T(8,128)(2,1)S(1)} %pad_maximum_fusion.10.refs_20_), channel_id=1, source_target_pairs={{0,4},{1,5},{2,6},{3,7},{12,8},{13,9},{14,10},{15,11},{16,20},{17,... | collective-permute-start | bytes 1179656 | tf_op jit(solution)/shard_map/ppermute | solution.py:32
  60.1 26.8 %collective-permute-start.11 = (bf16[8,64,1024]{2,1,0:T(8,128)(2,1)}, bf16[8,64,1024]{2,1,0:T(8,128)(2,1)}, u32[]{:S(2)}, u32[]{:S(2)}) collective-permute-start(bf16[8,64,1024]{2,1,0:T(8,128)(2,1)} %pad_maximum_fusion), channel_id=1, source_target_pairs={{0,4},{1,5},{2,6},{3,7},{12,8},{13,9},{14,10},{15,11},{16,20},{17,... | collective-permute-start | bytes 3145736 | tf_op jit(solution)/shard_map/ppermute | solution.py:32
  69.1 20.4 %collective-permute-start.13 = (bf16[4,64,1792]{2,1,0:T(8,128)(2,1)}, bf16[4,64,1792]{2,1,0:T(8,128)(2,1)}, u32[]{:S(2)}, u32[]{:S(2)}) collective-permute-start(bf16[4,64,1792]{2,1,0:T(8,128)(2,1)} %collective-permute-done.5.refs_3_), channel_id=1, source_target_pairs={{4,0},{5,1},{6,2},{7,3},{8,12},{9,13},{10,14},{11,15},{20,16},{21,... | collective-permute-start | bytes 2752520 | tf_op jit(solution)/shard_map/ppermute | solution.py:32
  72.2 14.8 %collective-permute-start.12 = (bf16[8,64,768]{2,1,0:T(8,128)(2,1)}, bf16[8,64,768]{2,1,0:T(8,128)(2,1)}, u32[]{:S(2)}, u32[]{:S(2)}) collective-permute-start(bf16[8,64,768]{2,1,0:T(8,128)(2,1)} %pad_maximum_fusion.2), channel_id=1, source_target_pairs={{4,8},{5,9},{6,10},{7,11},{8,4},{9,5},{10,6},{11,7},{20,24},{21,25... | collective-permute-start | bytes 2359304 | tf_op jit(solution)/shard_map/ppermute | solution.py:32
  102.2 22.3 %collective-permute-start.22 = (bf16[8,64,1024]{2,1,0:T(8,128)(2,1)}, bf16[8,64,1024]{2,1,0:T(8,128)(2,1)S(1)}, u32[]{:S(2)}, u32[]{:S(2)}) collective-permute-start(bf16[8,64,1024]{2,1,0:T(8,128)(2,1)} %get-tuple-element.125), channel_id=1, source_target_pairs={{4,0},{5,1},{6,2},{7,3},{8,12},{9,13},{10,14},{11,15},{20,16},{21,... | collective-permute-start | bytes 3145736 | tf_op jit(solution)/shard_map/ppermute | solution.py:32
  107.7 20.8 %collective-permute-start.17 = (bf16[2,64,1792]{2,1,0:T(8,128)(2,1)}, bf16[2,64,1792]{2,1,0:T(8,128)(2,1)S(1)}, u32[]{:S(2)}, u32[]{:S(2)}) collective-permute-start(bf16[2,64,1792]{2,1,0:T(8,128)(2,1)} %get-tuple-element.111), channel_id=1, source_target_pairs={{0,3},{1,0},{2,1},{3,2},{4,7},{5,4},{6,5},{7,6},{8,11},{9,8},{10,9... | collective-permute-start | bytes 1376264 | tf_op jit(solution)/shard_map/ppermute | solution.py:32
  114.0 20.5 %collective-permute-start.18 = (bf16[2,64,1792]{2,1,0:T(8,128)(2,1)}, bf16[2,64,1792]{2,1,0:T(8,128)(2,1)S(1)}, u32[]{:S(2)}, u32[]{:S(2)}) collective-permute-start(bf16[2,64,1792]{2,1,0:T(8,128)(2,1)} %get-tuple-element.113), channel_id=1, source_target_pairs={{0,1},{1,2},{2,3},{3,0},{4,5},{5,6},{6,7},{7,4},{8,9},{9,10},{10,1... | collective-permute-start | bytes 1376264 | tf_op jit(solution)/shard_map/ppermute | solution.py:32
  115.3 19.2 %collective-permute-start.16 = (bf16[2,64,2560]{2,1,0:T(8,128)(2,1)S(1)}, bf16[2,64,2560]{2,1,0:T(8,128)(2,1)S(1)}, u32[]{:S(2)}, u32[]{:S(2)}) collective-permute-start(bf16[2,64,2560]{2,1,0:T(8,128)(2,1)S(1)} %pad_maximum_fusion.4), channel_id=1, source_target_pairs={{4,8},{5,9},{6,10},{7,11},{8,4},{9,5},{10,6},{11,7},{20,24},{21,25... | collective-permute-start | bytes 1966088 | tf_op jit(solution)/shard_map/ppermute | solution.py:32
  116.2 18.3 %collective-permute-start.15 = (bf16[2,64,1792]{2,1,0:T(8,128)(2,1)S(1)}, bf16[2,64,1792]{2,1,0:T(8,128)(2,1)S(1)}, u32[]{:S(2)}, u32[]{:S(2)}) collective-permute-start(bf16[2,64,1792]{2,1,0:T(8,128)(2,1)S(1)} %copy-done.17), channel_id=1, source_target_pairs={{0,4},{1,5},{2,6},{3,7},{12,8},{13,9},{14,10},{15,11},{16,20},{17,... | collective-permute-start | bytes 1376264 | tf_op jit(solution)/shard_map/ppermute | solution.py:32
  128.5 12.9 %collective-permute-start.24 = (bf16[2,64,1024]{2,1,0:T(8,128)(2,1)S(1)}, bf16[2,64,1024]{2,1,0:T(8,128)(2,1)S(1)}, u32[]{:S(2)}, u32[]{:S(2)}) collective-permute-start(bf16[2,64,1024]{2,1,0:T(8,128)(2,1)S(1)} %maximum_select_fusion.2), channel_id=1, source_target_pairs={{0,2},{1,3},{2,0},{3,1},{4,6},{5,7},{6,4},{7,5},{8,10},{9,11},{10,... | collective-permute-start | bytes 786440 | tf_op jit(solution)/shard_map/ppermute | solution.py:32
  134.7 26.1 %collective-permute-start.20 = (bf16[2,64,2560]{2,1,0:T(8,128)(2,1)S(1)}, bf16[2,64,2560]{2,1,0:T(8,128)(2,1)S(1)}, u32[]{:S(2)}, u32[]{:S(2)}) collective-permute-start(bf16[2,64,2560]{2,1,0:T(8,128)(2,1)S(1)} %add_convert_fusion.1), channel_id=1, source_target_pairs={{0,4},{1,5},{2,6},{3,7},{4,0},{5,1},{6,2},{7,3},{8,12},{9,13},{10,... | collective-permute-start | bytes 1966088 | tf_op jit(solution)/shard_map/ppermute | solution.py:32
  135.0 25.8 %collective-permute-start.19 = (bf16[2,64,2560]{2,1,0:T(8,128)(2,1)S(1)}, bf16[2,64,2560]{2,1,0:T(8,128)(2,1)S(1)}, u32[]{:S(2)}, u32[]{:S(2)}) collective-permute-start(bf16[2,64,2560]{2,1,0:T(8,128)(2,1)S(1)} %pad_maximum_fusion.5), channel_id=1, source_target_pairs={{4,8},{5,9},{6,10},{7,11},{8,4},{9,5},{10,6},{11,7},{20,24},{21,25... | collective-permute-start | bytes 1966088 | tf_op jit(solution)/shard_map/ppermute | solution.py:32
  147.2 13.6 %collective-permute-start.21 = (bf16[2,64,1792]{2,1,0:T(8,128)(2,1)S(1)}, bf16[2,64,1792]{2,1,0:T(8,128)(2,1)S(1)}, u32[]{:S(2)}, u32[]{:S(2)}) collective-permute-start(bf16[2,64,1792]{2,1,0:T(8,128)(2,1)S(1)} %copy-done.26), channel_id=1, source_target_pairs={{0,2},{1,3},{2,0},{3,1},{4,6},{5,7},{6,4},{7,5},{8,10},{9,11},{10,... | collective-permute-start | bytes 1376264 | tf_op jit(solution)/shard_map/ppermute | solution.py:32
  160.8 13.0 %collective-permute-start.32 = (f32[64,256]{1,0:T(8,128)S(1)}, f32[64,256]{1,0:T(8,128)S(1)}, u32[]{:S(2)}, u32[]{:S(2)}) collective-permute-start(f32[64,256]{1,0:T(8,128)S(1)} %add.200), channel_id=1, source_target_pairs={{0,128},{16,144},{32,160},{48,176},{64,192},{80,208},{96,224},{112... | collective-permute-start | bytes 196616 | tf_op jit(solution)/shard_map/ppermute | solution.py:36
  165.4 11.8 %collective-permute-start.29 = (bf16[2,16,2560]{2,1,0:T(8,128)(2,1)S(1)}, bf16[2,16,2560]{2,1,0:T(8,128)(2,1)S(1)}, u32[]{:S(2)}, u32[]{:S(2)}) collective-permute-start(bf16[2,16,2560]{2,1,0:T(8,128)(2,1)S(1)} %get-tuple-element.162), channel_id=1, source_target_pairs={{0,3},{1,0},{2,1},{3,2},{4,7},{5,4},{6,5},{7,6},{8,11},{9,8},{10,9... | collective-permute-start | bytes 491528 | tf_op jit(solution)/shard_map/ppermute | solution.py:32
  (48 other events, 438.9 us)
